TPU v7x, 128 devices: a whole 4x4x4 slice. The times are simulated.
128 devices in a mesh: tm: 16 (over y_lo, x, core), head: 8 (over z, y_hi).
Axes of the slice: x: 4, y: 4 (y_hi: 2, y_lo: 2; y = y_hi * 2 + y_lo), z: 4, core: 2. Of those that a mesh axis runs over, the one named last changes fastest.
Arguments:
- queries: bfloat16 [32768, 3072], P('tm', 'head'), may hold values from -8 to 8
- keys: bfloat16 [32768, 3072], P('tm', 'head'), may hold values from -8 to 8
- values: bfloat16 [32768, 3072], P('tm', 'head'), may hold values from -6 to 6
- right_blocks: bfloat16 [24, 128, 128], P('head'), may hold values from -0.5 to 0.5
- left_blocks: bfloat16 [24, 128, 128], P('head'), may hold values from -0.5 to 0.5
- block_perm: int32 [24], replicated, may hold values from 0 to 23, each once
- reach: int32 [24], replicated, may hold values from 0 to 2, as said below
- grad_out: bfloat16 [32768, 3072], P('tm', 'head'), may hold values from -6 to 6
Outputs:
- projected: bfloat16 [32768, 3072], P('tm', 'head')
- d_queries: bfloat16 [32768, 3072], P('tm', 'head')
- d_keys: bfloat16 [32768, 3072], P('tm', 'head')
- d_values: bfloat16 [32768, 3072], P('tm', 'head')
- d_right: float32 [24, 128, 128], P('head')
- d_left: float32 [24, 128, 128], P('head')
Inputs may be any that keep to these rules, and one draw needn't show every extreme that they name: At least one head has reach 2. `block_perm`: each block number once.
All inputs are finite; a program needn't handle non-finite values.
Results may differ from a plain program's by a relative error of at most 0.023.
Values may be sent and summed in bfloat16 or wider, within the bound.
No kernel may reach another device: no remote copies, remote signals or barrier semaphores. Data moves between devices by JAX's collectives and lax.ppermute only.
A program may use at most 192 MiB of HBM per device.

v0:
```python
import jax
import jax.numpy as jnp
from jax import lax
from jax.sharding import PartitionSpec as P

NB = 24
BLK = 128
TILE = 128
RADIUS = 2
FR_DEV = 4
NTILE = 4


def padded(block, sides, width):
    for axis, dim in sides:
        count = lax.axis_size(axis)
        forward = [(i, i + 1) for i in range(count - 1)]
        backward = [(target, source) for source, target in forward]
        low = lax.ppermute(
            lax.slice_in_dim(block, block.shape[dim] - width, None, axis=dim), axis, forward
        )
        high = lax.ppermute(lax.slice_in_dim(block, 0, width, axis=dim), axis, backward)
        block = jnp.concatenate([low, block, high], axis=dim)
    return block


def shifted(x, axis, by):
    size = lax.axis_size(axis)
    pairs = [(i, i + by) for i in range(size) if 0 <= i + by < size]
    return lax.ppermute(x, axis, pairs)


def frame_mask(reach_heads, frames_q, frames_k, total_frames):
    gap = jnp.abs(frames_q[:, None] - frames_k[None, :])
    valid_q = (frames_q >= 0) & (frames_q < total_frames)
    valid_k = (frames_k >= 0) & (frames_k < total_frames)
    inside = valid_q[:, None] & valid_k[None, :]
    return (gap[None, :, :] <= reach_heads[:, None, None]) & inside[None, :, :]


def frame_list(first, count):
    return first + jnp.arange(count * TILE, dtype=jnp.int32) // TILE


def to_tiles(rows_array, local_heads):
    shaped = rows_array.reshape(FR_DEV, NTILE, TILE, local_heads, BLK)
    return jnp.transpose(shaped, (1, 3, 0, 2, 4))


def from_tiles(tiled, local_heads):
    shaped = tiled.reshape(NTILE, local_heads, FR_DEV, TILE, BLK)
    return jnp.transpose(shaped, (2, 0, 3, 1, 4)).reshape(FR_DEV * NTILE * TILE, local_heads * BLK)


def flat_rows(block):
    return block.reshape(block.shape[0], block.shape[1] * block.shape[2], block.shape[3])


def flat_stats(block):
    return block.reshape(block.shape[0], block.shape[1] * block.shape[2])


def scores(q_rows, k_rows, scale):
    return jnp.einsum("hqd,hkd->hqk", q_rows, k_rows, preferred_element_type=jnp.float32) * scale


def attend(q_rows, k_rows, v_rows, allowed, scale):
    s = scores(q_rows, k_rows, scale)
    top = jnp.max(jnp.where(allowed, s, -jnp.inf), axis=2, keepdims=True)
    total = jnp.sum(jnp.where(allowed, jnp.exp(s - top), 0.0), axis=2, keepdims=True)
    lse = top + jnp.log(total)
    probs = jnp.where(allowed, jnp.exp(s - lse), 0.0).astype(jnp.bfloat16)
    out = jnp.einsum("hqk,hkd->hqd", probs, v_rows, preferred_element_type=jnp.float32)
    return (out.astype(jnp.bfloat16), lse[:, :, 0])


def probs_again(q_rows, k_rows, allowed, lse, scale):
    s = scores(q_rows, k_rows, scale)
    return jnp.where(allowed, jnp.exp(s - lse[:, :, None]), 0.0)


def score_grads(probs, d_rows, v_rows, delta, scale):
    dp = jnp.einsum("hqd,hkd->hqk", d_rows, v_rows, preferred_element_type=jnp.float32)
    return (probs * (dp - delta[:, :, None]) * scale).astype(jnp.bfloat16)


def on_device(queries, keys, values, right_blocks, left_blocks, block_perm, reach, grad_out):
    rows, width = queries.shape
    local_heads = width // BLK
    n_head = lax.axis_size("head")
    piece = BLK // n_head
    scale = BLK ** (-0.5)
    span = FR_DEV + 2 * RADIUS
    total_frames = FR_DEV * lax.axis_size("tm")
    frame_base = lax.axis_index("tm") * FR_DEV
    head_reach = lax.dynamic_slice_in_dim(reach, lax.axis_index("head") * local_heads, local_heads)
    q_tiles = to_tiles(queries, local_heads)
    pair = jnp.stack([to_tiles(keys, local_heads), to_tiles(values, local_heads)])
    pair_ext = padded(pair, (("tm", 3),), RADIUS)
    k_ext = pair_ext[0]
    v_ext = pair_ext[1]
    own_frames = frame_list(frame_base, FR_DEV)
    ext_frames = frame_list(frame_base - RADIUS, span)
    near = frame_mask(head_reach, own_frames, ext_frames, total_frames)

    def forward_tile(items):
        q_block, k_block, v_block = items
        return attend(flat_rows(q_block), flat_rows(k_block), flat_rows(v_block), near, scale)

    attn_tiles, lse_tiles = lax.map(forward_tile, (q_tiles, k_ext, v_ext))
    attn_flat = from_tiles(attn_tiles, local_heads)
    attn_rows = attn_flat.reshape(rows, local_heads, BLK)
    columns = jnp.arange(width, dtype=jnp.int32)
    out_block = columns % NB
    out_lane = columns // NB
    picked = jnp.sum(
        jnp.where(
            jnp.arange(NB, dtype=jnp.int32)[None, :] == out_block[:, None], block_perm[None, :], 0
        ),
        axis=1,
    )
    source = picked * piece + out_lane
    placer = (columns[:, None] == source[None, :]).astype(jnp.bfloat16)
    r4 = right_blocks.reshape(local_heads, BLK, n_head, piece)
    mixed = jnp.einsum("nbi,bisl->sbln", attn_rows, r4, preferred_element_type=jnp.float32).astype(
        jnp.bfloat16
    )
    mixed = mixed.reshape(n_head, local_heads * piece, rows)
    arrived = lax.all_to_all(mixed, "head", split_axis=0, concat_axis=0, tiled=True).reshape(
        width, rows
    )
    placed_t = jnp.dot(placer.T, arrived, preferred_element_type=jnp.float32).astype(jnp.bfloat16)
    placed3 = placed_t.reshape(local_heads, BLK, rows)
    projected = jnp.einsum("cin,cio->nco", placed3, left_blocks, preferred_element_type=jnp.float32)
    projected = projected.astype(jnp.bfloat16).reshape(rows, width)
    cot3 = grad_out.reshape(rows, local_heads, BLK)
    d_placed = jnp.einsum(
        "nco,cio->cin", cot3, left_blocks, preferred_element_type=jnp.float32
    ).astype(jnp.bfloat16)
    left_term = jnp.einsum("cin,nco->cio", placed3, cot3, preferred_element_type=jnp.float32)
    d_arrived = jnp.dot(
        placer, d_placed.reshape(width, rows), preferred_element_type=jnp.float32
    ).astype(jnp.bfloat16)
    d_mixed = lax.all_to_all(
        d_arrived.reshape(n_head, local_heads * piece, rows),
        "head",
        split_axis=0,
        concat_axis=0,
        tiled=True,
    )
    d4 = d_mixed.reshape(n_head, local_heads, piece, rows)
    d_attn = jnp.einsum("sbln,bisl->nbi", d4, r4, preferred_element_type=jnp.float32).astype(
        jnp.bfloat16
    )
    right_term = jnp.einsum(
        "nbi,sbln->bisl", attn_rows, d4, preferred_element_type=jnp.float32
    ).reshape(local_heads, BLK, BLK)
    right_sum, left_sum = (
        lax.psum(right_term.astype(jnp.bfloat16), "tm").astype(jnp.float32),
        lax.psum(left_term.astype(jnp.bfloat16), "tm").astype(jnp.float32),
    )
    norm = float(rows * lax.axis_size("tm")) ** (-0.5)
    d_right = right_sum * norm
    d_left = left_sum * norm
    delta = jnp.sum(d_attn.astype(jnp.float32) * attn_rows.astype(jnp.float32), axis=2)
    delta_tiles = jnp.transpose(delta.reshape(FR_DEV, NTILE, TILE, local_heads), (1, 3, 0, 2))
    lse_shaped = lse_tiles.reshape(NTILE, local_heads, FR_DEV, TILE)
    d_tiles = to_tiles(d_attn.reshape(rows, width), local_heads)

    def backward_tile(items):
        q_block, d_block, k_block, v_block, lse_block, delta_block = items
        q_rows = flat_rows(q_block)
        d_rows = flat_rows(d_block)
        k_rows = flat_rows(k_block)
        probs = probs_again(q_rows, k_rows, near, flat_stats(lse_block), scale)
        grads = score_grads(probs, d_rows, flat_rows(v_block), flat_stats(delta_block), scale)
        d_query = jnp.einsum(
            "hqk,hkd->hqd", grads, k_rows, preferred_element_type=jnp.float32
        ).astype(jnp.bfloat16)
        d_key = jnp.einsum("hqk,hqd->hkd", grads, q_rows, preferred_element_type=jnp.float32)
        d_value = jnp.einsum(
            "hqk,hqd->hkd", probs.astype(jnp.bfloat16), d_rows, preferred_element_type=jnp.float32
        )
        return (d_query, jnp.stack([d_key, d_value]))

    dq_tiles, kv_tiles = lax.map(
        backward_tile, (q_tiles, d_tiles, k_ext, v_ext, lse_shaped, delta_tiles)
    )
    kv_grads = kv_tiles.reshape(NTILE, 2, local_heads, span, TILE, BLK)
    from_above = shifted(kv_grads[:, :, :, :RADIUS].astype(jnp.bfloat16), "tm", -1).astype(
        jnp.float32
    )
    from_below = shifted(kv_grads[:, :, :, RADIUS + FR_DEV :].astype(jnp.bfloat16), "tm", 1).astype(
        jnp.float32
    )
    own = kv_grads[:, :, :, RADIUS : RADIUS + FR_DEV]
    own = own.at[:, :, :, FR_DEV - RADIUS :].add(from_above)
    own = own.at[:, :, :, :RADIUS].add(from_below)
    own = own.astype(jnp.bfloat16)
    d_queries = from_tiles(dq_tiles, local_heads)
    d_keys = from_tiles(own[:, 0], local_heads)
    d_values = from_tiles(own[:, 1], local_heads)
    return (projected, d_queries, d_keys, d_values, d_right, d_left)


def solution(mesh):
    in_specs = (
        P("tm", "head"),
        P("tm", "head"),
        P("tm", "head"),
        P("head", None, None),
        P("head", None, None),
        P(),
        P(),
        P("tm", "head"),
    )
    out_specs = (
        P("tm", "head"),
        P("tm", "head"),
        P("tm", "head"),
        P("tm", "head"),
        P("head", None, None),
        P("head", None, None),
    )
    return jax.shard_map(
        on_device, mesh=mesh, in_specs=in_specs, out_specs=out_specs, check_vma=False
    )
```

profile of v0, /device:TPU:16, one launch (start us, length us, event | category | flops | bytes accessed | tf_op | source)
XLA Modules:
  0.0 382.7 jit_solution(6202498669068435902)
XLA Ops:
  7.2 1.7 copy.65
  10.1 3.1 copy.66
  13.2 2.8 reshape.347
  16.1 3.5 fusion.25
  19.6 2.9 collective-permute-start
  23.9 1.7 copy.75
  26.3 2.2 convolution_convert_fusion.1
  28.4 8.8 %all-to-all-start.1 = ((bf16[8,48,2048]{2,1,0:T(8,128)(2,1)}), bf16[8,48,2048]{2,1,0:T(8,128)(2,1)}, u32[]{:S(2)}, u32[]{:S(2)}) async-start(bf16[8,48,2048]{2,1,0:T(8,128)(2,1)} %bitcast.21), calls=%async_computation.1 | async-start | bytes 3145728 | tf_op jit(solution)/shard_map/all_to_all | solution.py:144
  39.4 2.5 copy.67
  42.6 7.1 %pad_maximum_fusion = bf16[2,4,3,8,128,128]{4,1,3,5,2,0:T(4,128)(2,1)S(1)} fusion(bf16[2,4,3,2,128,128]{4,1,3,5,2,0:T(4,128)(2,1)} %collective-permute-done.1, bf16[1,4,3,4,128,128]{4,1,3,5,2,0:T(4,128)(2,1)} %bitcast.199, bf16[1,4,3,4,128,128]{4,1,3,5,2,0:T(4,128)(2,1)} %bitcast.197, bf16[2,4,3,2,128,128]{4,1,3,5,2,0:T(4,128)(2,1)} %collective-permute-done), kind=kLoop, calls=%fused_computation.40 | loop fusion | flops 9437184 | bytes 12582912 | tf_op jit(solution)/shard_map/concatenate | solution.py:23
  49.7 4.1 %slice_bitcast_fusion = (bf16[4,3,8,128,128]{3,0,2,4,1:T(4,128)(2,1)}, bf16[4,3,8,128,128]{3,0,2,4,1:T(4,128)(2,1)}) fusion(bf16[2,4,3,8,128,128]{4,1,3,5,2,0:T(4,128)(2,1)S(1)} %pad_maximum_fusion), kind=kLoop, calls=%fused_computation.45 | loop fusion | bytes 12582912 | tf_op jit(solution)/shard_map/squeeze | solution.py:101
  53.9 6.2 %copy.69 = bf16[4,3,8,128,128]{4,3,2,1,0:T(8,128)(2,1)} copy(bf16[4,3,8,128,128]{3,0,2,4,1:T(4,128)(2,1)} %get-tuple-element.295) | data formatting | bytes 6291456
  60.1 6.2 %copy.68 = bf16[4,3,8,128,128]{4,3,2,1,0:T(8,128)(2,1)} copy(bf16[4,3,8,128,128]{3,0,2,4,1:T(4,128)(2,1)} %get-tuple-element.296) | data formatting | bytes 6291456
  67.7 42.0 %while.28 = (s32[]{:T(128)}, bf16[4,3,512,128]{3,2,1,0:T(8,128)(2,1)}, f32[4,3,512]{2,1,0:T(4,128)S(1)}, bf16[4,3,4,128,128]{4,3,2,1,0:T(8,128)(2,1)}, bf16[4,3,...) while((s32[]{:T(128)}, ...), condition=%wide.region_4.5_spmd.clone, body=%wide.region_1.4_spmd.clone.sunk | while | flops 832240128 | bytes 33087648 | solution.py:110
  70.2 2.0 select_reduce_fusion.5
  72.2 2.7 select_reduce_fusion.6
  74.9 3.2 fusion.96
  80.7 2.0 select_reduce_fusion.5
  82.7 2.7 select_reduce_fusion.6
  85.4 3.2 fusion.96
  91.2 2.0 select_reduce_fusion.5
  93.2 2.7 select_reduce_fusion.6
  95.9 3.2 fusion.96
  101.7 2.0 select_reduce_fusion.5
  103.7 2.7 select_reduce_fusion.6
  106.4 3.2 fusion.96
  109.7 2.7 copy.70
  112.4 3.8 multiply_reduce_fusion
  116.3 2.8 copy.116
  121.2 7.2 %all-to-all-start = ((bf16[8,48,2048]{2,1,0:T(8,128)(2,1)}), bf16[8,48,2048]{2,1,0:T(8,128)(2,1)}, u32[]{:S(2)}, u32[]{:S(2)}) async-start(bf16[8,48,2048]{2,1,0:T(8,128)(2,1)} %bitcast.206), calls=%async_computation | async-start | bytes 3145728 | tf_op jit(solution)/shard_map/all_to_all | solution.py:129
  128.4 10.0 %all-reduce.3.cloned.1.call-start = ((), (), s32[]{:S(2)}) async-start(), calls=%async_computation.2 | async-start | bytes 393216 | tf_op jit(solution)/shard_map/psum | solution.py:159
  139.8 56.8 %while.29 = (s32[]{:T(128)}, bf16[4,3,512,128]{3,2,1,0:T(8,128)(2,1)}, f32[4,2,3,1024,128]{4,3,2,1,0:T(8,128)}, bf16[4,3,4,128,128]{4,3,2,1,0:T(8,128)(2,1)}, bf...) while((s32[]{:T(128)}, ...), condition=%wide.region_7.8_spmd.clone, body=%wide.region_6.7_spmd.clone.sunk | while | flops 2037841920 | bytes 52103348 | solution.py:186
  143.5 2.6 fusion.109
  146.2 3.0 multiply_convert_fusion.2
  149.2 1.7 fusion.108
  152.2 1.8 fusion.110
  157.7 2.6 fusion.109
  160.3 3.0 multiply_convert_fusion.2
  163.3 1.7 fusion.108
  166.3 1.9 fusion.110
  171.9 2.6 fusion.109
  174.5 3.0 multiply_convert_fusion.2
  177.5 1.7 fusion.108
  180.5 1.9 fusion.110
  186.2 2.6 fusion.109
  188.8 3.0 multiply_convert_fusion.2
  191.8 1.7 fusion.108
  194.8 1.9 fusion.110
  196.7 15.1 %copy.85 = f32[4,2,3,8,128,128]{4,0,3,5,2,1:T(4,128)} copy(f32[4,2,3,8,128,128]{5,4,3,2,1,0:T(8,128)} %bitcast.200) | data formatting | bytes 25165824 | tf_op jit(solution)/shard_map/reshape | solution.py:189
  211.8 10.4 %convert.4 = bf16[4,2,3,8,128,128]{4,0,3,5,2,1:T(4,128)(2,1)} convert(f32[4,2,3,8,128,128]{4,0,3,5,2,1:T(4,128)} %copy.85) | non-fusion elementwise | flops 3145728 | bytes 18874368 | tf_op jit(solution)/shard_map/convert.1
  222.2 4.9 %fusion.48 = (bf16[4,2,3,2,128,128]{4,0,3,5,2,1:T(4,128)(2,1)}, bf16[4,2,3,2,128,128]{4,0,3,5,2,1:T(4,128)(2,1)}) fusion(bf16[4,2,3,8,128,128]{4,0,3,5,2,1:T(4,128)(2,1)} %convert.4), kind=kLoop, calls=%fused_computation.104 | loop fusion | bytes 6291456 | tf_op jit(solution)/shard_map/slice | solution.py:193
  228.5 6.7 %slice.123 = f32[4,2,3,4,128,128]{4,0,3,5,2,1:T(4,128)} slice(f32[4,2,3,8,128,128]{4,0,3,5,2,1:T(4,128)} %copy.85), slice={[0:4], [0:2], [0:3], [2:6], [0:128], [0:128]} | slice | bytes 12582912 | tf_op jit(solution)/shard_map/slice | solution.py:196
  235.1 7.0 %collective-permute-start.3 = (bf16[4,2,3,2,128,128]{4,0,3,5,2,1:T(4,128)(2,1)}, bf16[4,2,3,2,128,128]{4,0,3,5,2,1:T(4,128)(2,1)}, u32[]{:S(2)}, u32[]{:S(2)}) collective-permute-start(bf16[4,2,3,2,128,128]{4,0,3,5,2,1:T(4,128)(2,1)} %get-tuple-element.293), channel_id=1, source_target_pairs={{0,8},{8,16},{16,24},{24,32},{32,40},{40,48},{48,56},{56,64},{64,7... | collective-permute-start | bytes 4718600 | tf_op jit(solution)/shard_map/ppermute | solution.py:30
  242.1 2.1 fusion.28
  249.2 2.4 convolution_convert_fusion.4
  251.7 1.8 convolution_convert_fusion.3
  253.4 2.7 copy.91
  257.4 4.9 %fusion.24 = f32[4,2,3,4,128,128]{4,0,3,5,2,1:T(4,128)} fusion(f32[4,2,3,4,128,128]{4,0,3,5,2,1:T(4,128)} %slice.123, f32[4,2,3,8,128,128]{4,0,3,5,2,1:T(4,128)} %copy.85, bf16[4,2,3,2,128,128]{4,0,3,5,2,1:T(4,128)(2,1)} %collective-permute-done.2), kind=kLoop, calls=%fused_computation.44 | loop fusion | flops 1572864 | bytes 7864320 | tf_op jit(solution)/shard_map/scatter-add | solution.py:197
  262.3 4.9 %fusion.23 = f32[4,2,3,4,128,128]{4,0,3,5,2,1:T(4,128)} fusion(f32[4,2,3,4,128,128]{4,0,3,5,2,1:T(4,128)} %fusion.24, bf16[4,2,3,2,128,128]{4,0,3,5,2,1:T(4,128)(2,1)} %collective-permute-done.3), kind=kLoop, calls=%fused_computation.42 | loop fusion | flops 1572864 | bytes 7864320 | tf_op jit(solution)/shard_map/scatter-add | solution.py:198
  267.1 3.9 %convert_element_type.88 = bf16[4,2,3,4,128,128]{4,0,3,5,2,1:T(4,128)(2,1)S(1)} convert(f32[4,2,3,4,128,128]{4,0,3,5,2,1:T(4,128)} %fusion.23) | non-fusion elementwise | flops 1572864 | bytes 9437184 | tf_op jit(solution)/shard_map/convert_element_type | solution.py:199
  271.0 2.2 slice_bitcast_fusion.2
  273.2 2.9 reshape.364
  280.4 93.4 %all-reduce.3.cloned.1.call-done = (bf16[3,128,128]{2,1,0:T(8,128)(2,1)}, bf16[3,128,128]{2,1,0:T(8,128)(2,1)}) async-done(((bf16[3,128,128]{2,1,0:T(8,128)(2,1)}, bf16[3,128,128]{2,1,0:T(8,128)(2,1)}), (bf16[3,128,128]{2,1,0:T(8,128)(2,1)}, bf16[3,128,128]{2,1,0:T(8,128)(2,1)})) %all-reduce.3.cloned.1.call-update) | async-done | bytes 196624 | tf_op jit(solution)/shard_map/psum | solution.py:159
  373.9 1.7 convert_multiply_fusion
  (109 shorter events, 52.5 us)
Async XLA Ops:
  7.2 18.5 %copy-start = (bf16[3,128,128]{2,1,0:T(8,128)(2,1)S(1)}, bf16[3,128,128]{2,1,0:T(8,128)(2,1)}, u32[]{:S(2)}) copy-start(bf16[3,128,128]{2,1,0:T(8,128)(2,1)} %param.20) | copy-start | bytes 294916
  10.1 6.0 %copy-start.3 = (bf16[4,4,128,3,128]{2,1,0,4,3:T(4,128)(2,1)}, bf16[4,4,128,3,128]{2,1,0,4,3:T(4,128)(2,1)S(1)}, u32[]{:S(2)}) copy-start(bf16[4,4,128,3,128]{2,1,0,4,3:T(4,128)(2,1)S(1)} %reshape.346) | copy-start | bytes 4718596
  16.1 3.5 copy-start.4
  16.1 7.7 %copy-start.12 = (s32[24]{0:T(128)S(1)}, s32[24]{0:T(128)}, u32[]{:S(2)}) copy-start(s32[24]{0:T(128)} %param.21) | copy-start | bytes 292
  19.6 23.0 %collective-permute-start = (bf16[2,4,3,2,128,128]{4,1,3,5,2,0:T(4,128)(2,1)}, bf16[2,4,3,2,128,128]{4,1,3,5,2,0:T(4,128)(2,1)}, u32[]{:S(2)}, u32[]{:S(2)}) collective-permute-start(bf16[2,4,3,2,128,128]{4,1,3,5,2,0:T(4,128)(2,1)} %get-tuple-element.299), channel_id=1, source_target_pairs={{0,8},{8,16},{16,24},{24,32},{32,40},{40,48},{48,56},{56,64},{64,7... | collective-permute-start | bytes 4718600 | tf_op jit(solution)/shard_map/ppermute | solution.py:19
  22.5 20.1 %collective-permute-start.1 = (bf16[2,4,3,2,128,128]{4,1,3,5,2,0:T(4,128)(2,1)}, bf16[2,4,3,2,128,128]{4,1,3,5,2,0:T(4,128)(2,1)}, u32[]{:S(2)}, u32[]{:S(2)}) collective-permute-start(bf16[2,4,3,2,128,128]{4,1,3,5,2,0:T(4,128)(2,1)} %get-tuple-element.300), channel_id=1, source_target_pairs={{8,0},{16,8},{24,16},{32,24},{40,32},{48,40},{56,48},{64,56},{72,6... | collective-permute-start | bytes 4718600 | tf_op jit(solution)/shard_map/ppermute | solution.py:22
  23.9 2.3 copy-start.10
  25.7 2.8 copy-start.1
  28.4 8.9 %copy-start.9 = (bf16[3,128,128]{2,1,0:T(8,128)(2,1)S(1)}, bf16[3,128,128]{2,1,0:T(8,128)(2,1)}, u32[]{:S(2)}) copy-start(bf16[3,128,128]{2,1,0:T(8,128)(2,1)} %param.19) | copy-start | bytes 294916
  28.4 9.0 %copy-start.8 = (bf16[2048,384]{1,0:T(8,128)(2,1)S(1)}, bf16[2048,384]{1,0:T(8,128)(2,1)}, u32[]{:S(2)}) copy-start(bf16[2048,384]{1,0:T(8,128)(2,1)} %param.16) | copy-start | bytes 4718596
  28.4 84.0 %all-to-all-start.1 = ((bf16[8,48,2048]{2,1,0:T(8,128)(2,1)}), bf16[8,48,2048]{2,1,0:T(8,128)(2,1)}, u32[]{:S(2)}, u32[]{:S(2)}) async-start(bf16[8,48,2048]{2,1,0:T(8,128)(2,1)} %bitcast.21), calls=%async_computation.1 | async-start | bytes 3145728 | tf_op jit(solution)/shard_map/all_to_all | solution.py:144
  39.4 2.5 copy-start.13
  116.2 2.9 copy-start.6
  121.2 128.0 %all-to-all-start = ((bf16[8,48,2048]{2,1,0:T(8,128)(2,1)}), bf16[8,48,2048]{2,1,0:T(8,128)(2,1)}, u32[]{:S(2)}, u32[]{:S(2)}) async-start(bf16[8,48,2048]{2,1,0:T(8,128)(2,1)} %bitcast.206), calls=%async_computation | async-start | bytes 3145728 | tf_op jit(solution)/shard_map/all_to_all | solution.py:129
  128.4 245.5 %all-reduce.3.cloned.1.call-start = ((), (), s32[]{:S(2)}) async-start(), calls=%async_computation.2 | async-start | bytes 393216 | tf_op jit(solution)/shard_map/psum | solution.py:159
  227.0 15.1 %copy-start.7 = (bf16[4,3,4,128,128]{4,3,0,2,1:T(8,128)(2,1)S(1)}, bf16[4,3,4,128,128]{4,3,0,2,1:T(8,128)(2,1)}, u32[]{:S(2)}) copy-start(bf16[4,3,4,128,128]{4,3,0,2,1:T(8,128)(2,1)} %copy.70) | copy-start | bytes 4718596
  227.0 30.4 %collective-permute-start.2 = (bf16[4,2,3,2,128,128]{4,0,3,5,2,1:T(4,128)(2,1)}, bf16[4,2,3,2,128,128]{4,0,3,5,2,1:T(4,128)(2,1)}, u32[]{:S(2)}, u32[]{:S(2)}) collective-permute-start(bf16[4,2,3,2,128,128]{4,0,3,5,2,1:T(4,128)(2,1)} %get-tuple-element.294), channel_id=1, source_target_pairs={{8,0},{16,8},{24,16},{32,24},{40,32},{48,40},{56,48},{64,56},{72,6... | collective-permute-start | bytes 4718600 | tf_op jit(solution)/shard_map/ppermute | solution.py:30
  235.1 27.2 %collective-permute-start.3 = (bf16[4,2,3,2,128,128]{4,0,3,5,2,1:T(4,128)(2,1)}, bf16[4,2,3,2,128,128]{4,0,3,5,2,1:T(4,128)(2,1)}, u32[]{:S(2)}, u32[]{:S(2)}) collective-permute-start(bf16[4,2,3,2,128,128]{4,0,3,5,2,1:T(4,128)(2,1)} %get-tuple-element.293), channel_id=1, source_target_pairs={{0,8},{8,16},{16,24},{24,32},{32,40},{40,48},{48,56},{56,64},{64,7... | collective-permute-start | bytes 4718600 | tf_op jit(solution)/shard_map/ppermute | solution.py:30
  242.1 2.9 copy-start.5
  247.6 1.6 copy-start.11
  253.4 2.7 copy-start.2
Sparse Core Ops, SparseCore 0:
  257.5 116.3 all-reduce.2
where the time goes:
time: 390 us; the launch traced here: 383 us
  local copies, waits for them, and re-layouts  106 us (27%)
  waiting for transfers between devices  93.5 us (24%)
  matrix products  74.1 us (19%)
  other arithmetic  55.6 us (14%)
  starting transfers between devices  38.7 us (10%)
  between operations  14.6 us (4%)
    psum x1, waiting for transfers between devices, on_device(): lax.psum(right_term.astype(jnp.bfloat16), 'tm').astype(jnp.float32)  93.4 us
    unnamed x40, local copies, waits for them, and re-layouts  29.9 us
    dynamic_slice x16, local copies, waits for them, and re-layouts, on_device(): attn_tiles, lse_tiles = lax.map(forward_tile, (q_tiles, k_ext, v_ext))  20.6 us
    reshape x1, local copies, waits for them, and re-layouts, on_device(): kv_grads = kv_tiles.reshape(NTILE, 2, local_heads, span, TILE, BLK)  15.1 us
    dot_general x4, matrix products, attend(): jnp.einsum('hqk,hkd->hqd', probs, v_rows, preferred_element_type=jnp.floa...  12.9 us
    dot_general x8, matrix products, scores(): jnp.einsum('hqd,hkd->hqk', q_rows, k_rows, preferred_element_type=jnp.flo...  12.1 us
    dot_general x4, matrix products, score_grads(): jnp.einsum('hqd,hkd->hqk', d_rows, v_rows, preferred_element_type=jnp.flo...  12 us
    reduce_sum x4, other arithmetic, attend(): jnp.sum(jnp.where(allowed, jnp.exp(s - top), 0.0), axis=2, keepdims=True)  10.7 us
  transfers between devices with their start and end apart: 7, of which 1 were waited for; matrix products, arithmetic and copies ran while one was open for 56% of the time, Pallas kernels for 0%

commit v1 on v0

v1 whole, which is shorter than its diff:
```python
import functools

import jax
import jax.numpy as jnp
from jax import lax
from jax.experimental import pallas as pl
from jax.experimental.pallas import tpu as pltpu
from jax.sharding import PartitionSpec as P

NB = 24
BLK = 128
TILE = 128
RADIUS = 2
FR_DEV = 4
NTILE = 4
NF = 64
HL = 3
WID = HL * BLK
ROWS = FR_DEV * NTILE * TILE
COLS = FR_DEV * TILE
PIECE = 16
SCALE = BLK ** (-0.5)
LOG2E = 1.4426950408889634
NEG = -1e30
F32 = jnp.float32
BF16 = jnp.bfloat16
VMEM = 56 * 1024 * 1024

NN = (((1,), (0,)), ((), ()))
NT = (((1,), (1,)), ((), ()))
TN = (((0,), (0,)), ((), ()))


def dot(a, b, dims=NN):
    return lax.dot_general(a, b, dims, preferred_element_type=F32)


def params():
    return pltpu.CompilerParams(vmem_limit_bytes=VMEM, dimension_semantics=("arbitrary",))


def placer_of(perm_ref, flip):
    shape = (WID, 1) if flip else (1, WID)
    col = lax.broadcasted_iota(jnp.int32, shape, 0 if flip else 1)
    block = lax.rem(col, NB)
    lane = lax.div(col, NB)
    source = jnp.zeros(shape, jnp.int32)
    for b in range(NB):
        source = jnp.where(block == b, perm_ref[b] * PIECE, source)
    source = source + lane
    row = lax.broadcasted_iota(jnp.int32, (WID, WID), 1 if flip else 0)
    return jnp.where(row == source, 1.0, 0.0).astype(BF16)


def block_diag(blocks):
    rows = []
    for c in range(HL):
        parts = [blocks[c] if d == c else jnp.zeros((BLK, BLK), BF16) for d in range(HL)]
        rows.append(jnp.concatenate(parts, axis=1))
    return jnp.concatenate(rows, axis=0)


def piece_order():
    row = lax.broadcasted_iota(jnp.int32, (WID, WID), 0)
    col = lax.broadcasted_iota(jnp.int32, (WID, WID), 1)
    s = lax.div(col, HL * PIECE)
    rest = lax.rem(col, HL * PIECE)
    want = lax.div(rest, PIECE) * BLK + s * PIECE + lax.rem(rest, PIECE)
    return jnp.where(row == want, 1.0, 0.0).astype(BF16)


def prep_kernel(perm_ref, left_ref, right_ref, g_ref, w_ref, rb_ref, da_ref):
    @pl.when(pl.program_id(0) == 0)
    def _():
        w_ref[...] = dot(placer_of(perm_ref, False), block_diag(left_ref[...])).astype(BF16)
        rb_ref[...] = dot(block_diag(right_ref[...]), piece_order()).astype(BF16)

    g = g_ref[...].reshape(COLS, WID)
    da_ref[...] = dot(w_ref[...], g, NT).astype(BF16)


def whole(shape):
    return pl.BlockSpec(shape, lambda t: (0,) * len(shape))


def smem():
    return pl.BlockSpec(memory_space=pltpu.SMEM)


def tile_spec(frames):
    return pl.BlockSpec((frames, 1, TILE, WID), lambda t: (0, t, 0, 0))


def col_spec():
    return pl.BlockSpec((WID, COLS), lambda t: (0, t))


def prep(perm, left, right, g4):
    return pl.pallas_call(
        prep_kernel,
        grid=(NTILE,),
        in_specs=[smem(), whole((HL, BLK, BLK)), whole((HL, BLK, BLK)), tile_spec(FR_DEV)],
        out_specs=[whole((WID, WID)), whole((WID, WID)), col_spec()],
        out_shape=[
            jax.ShapeDtypeStruct((WID, WID), BF16),
            jax.ShapeDtypeStruct((WID, WID), BF16),
            jax.ShapeDtypeStruct((WID, ROWS), BF16),
        ],
        compiler_params=params(),
        cost_estimate=pl.CostEstimate(flops=10**9, bytes_accessed=4 * 10**6, transcendentals=0),
        name="prep",
    )(perm, left, right, g4)


def ext_rows(lo, own, hi, h, first, count):
    cols = slice(h * BLK, (h + 1) * BLK)
    parts = []
    for e in range(first, first + count):
        if e < RADIUS:
            parts.append(lo[e, 0, :, cols])
        elif e < RADIUS + FR_DEV:
            parts.append(own[e - RADIUS, 0, :, cols])
        else:
            parts.append(hi[e - RADIUS - FR_DEV, 0, :, cols])
    return jnp.concatenate(parts, axis=0)


SPAN = 6


def forward_kernel(
    reach_ref, q_ref, k_ref, v_ref, klo, khi, vlo, vhi, rb_ref, at_ref, p_ref, mix_ref
):
    base = lax.axis_index("tm") * FR_DEV
    head0 = lax.axis_index("head") * HL
    for h in range(HL):
        reach = reach_ref[head0 + h]
        cols = slice(h * BLK, (h + 1) * BLK)
        for pair in range(2):
            f0 = 2 * pair
            q = q_ref[f0 : f0 + 2, 0, :, cols].reshape(2 * TILE, BLK)
            k = ext_rows(klo, k_ref, khi, h, f0, SPAN)
            v = ext_rows(vlo, v_ref, vhi, h, f0, SPAN)
            s = dot(k, q, NT)
            halves = []
            for a in range(2):
                parts = []
                for j in range(5):
                    frame = base + f0 + a + j - RADIUS
                    ok = (abs(j - RADIUS) <= reach) & (frame >= 0) & (frame < NF)
                    bias = jnp.where(ok, 0.0, NEG)
                    e = a + j
                    piece = s[e * TILE : (e + 1) * TILE, a * TILE : (a + 1) * TILE]
                    parts.append(piece * (SCALE * LOG2E) + bias)
                x = jnp.concatenate(parts, axis=0)
                top = jnp.max(x, axis=0, keepdims=True)
                x = jnp.exp2(x - top)
                total = jnp.sum(x, axis=0, keepdims=True)
                x = (x * (1.0 / total)).astype(BF16)
                zero = jnp.zeros((TILE, TILE), BF16)
                halves.append(jnp.concatenate([x, zero] if a == 0 else [zero, x], axis=0))
            p = jnp.concatenate(halves, axis=1)
            p_ref[0, h, pair] = p
            at_ref[cols, f0 * TILE : (f0 + 2) * TILE] = dot(v, p, TN).astype(BF16)
    mix_ref[...] = dot(rb_ref[...], at_ref[...], TN).astype(BF16)


def forward(reach, q4, k4, v4, klo, khi, vlo, vhi, rb):
    return pl.pallas_call(
        forward_kernel,
        grid=(NTILE,),
        in_specs=[smem()]
        + [tile_spec(FR_DEV)] * 3
        + [tile_spec(RADIUS)] * 4
        + [whole((WID, WID))],
        out_specs=[
            col_spec(),
            pl.BlockSpec((1, HL, 2, SPAN * TILE, 2 * TILE), lambda t: (t, 0, 0, 0, 0)),
            col_spec(),
        ],
        out_shape=[
            jax.ShapeDtypeStruct((WID, ROWS), BF16),
            jax.ShapeDtypeStruct((NTILE, HL, 2, SPAN * TILE, 2 * TILE), BF16),
            jax.ShapeDtypeStruct((WID, ROWS), BF16),
        ],
        compiler_params=params(),
        cost_estimate=pl.CostEstimate(
            flops=6 * 10**9, bytes_accessed=20 * 10**6, transcendentals=4 * 10**6
        ),
        name="forward",
    )(reach, q4, k4, v4, klo, khi, vlo, vhi, rb)


def backward_kernel(
    q_ref, k_ref, v_ref, klo, khi, vlo, vhi, rb_ref, at_ref, p_ref, dm_ref,
    dq_ref, dk_ref, dv_ref, lo_ref, hi_ref, r_ref, acc_ref,
):
    t = pl.program_id(0)
    dat = dot(rb_ref[...], dm_ref[...]).astype(BF16)
    term = dot(at_ref[...], dm_ref[...], NT)

    @pl.when(t == 0)
    def _():
        acc_ref[...] = term

    @pl.when(t > 0)
    def _():
        acc_ref[...] += term

    for h in range(HL):
        cols = slice(h * BLK, (h + 1) * BLK)
        dat_h = dat[cols, :]
        delta = jnp.sum(dat_h.astype(F32) * at_ref[cols, :].astype(F32), axis=0, keepdims=True)
        dks, dvs = [], []
        for pair in range(2):
            f0 = 2 * pair
            lanes = slice(f0 * TILE, (f0 + 2) * TILE)
            q = q_ref[f0 : f0 + 2, 0, :, cols].reshape(2 * TILE, BLK)
            k = ext_rows(klo, k_ref, khi, h, f0, SPAN)
            v = ext_rows(vlo, v_ref, vhi, h, f0, SPAN)
            p = p_ref[0, h, pair]
            d_t = dat_h[:, lanes]
            dp = dot(v, d_t)
            grads = (p.astype(F32) * (dp - delta[:, lanes])).astype(BF16)
            dq = dot(grads, k, TN) * SCALE
            dq_ref[f0 : f0 + 2, 0, :, cols] = dq.astype(BF16).reshape(2, TILE, BLK)
            dks.append(dot(grads, q) * SCALE)
            dvs.append(dot(p, d_t, NT))
        for which, (low, high) in enumerate((dks, dvs)):
            own_ref = dk_ref if which == 0 else dv_ref
            for e in range(RADIUS):
                lo_ref[which, e, 0, :, cols] = low[e * TILE : (e + 1) * TILE].astype(BF16)
                hi_ref[which, e, 0, :, cols] = high[(e + 4) * TILE : (e + 5) * TILE].astype(BF16)
            for e in range(FR_DEV):
                own = low[(e + 2) * TILE : (e + 3) * TILE] + high[e * TILE : (e + 1) * TILE]
                own_ref[e, 0, :, cols] = own.astype(BF16)

    @pl.when(t == NTILE - 1)
    def _():
        full = dot(acc_ref[...].astype(BF16), piece_order(), NT)
        for b in range(HL):
            r_ref[b] = full[b * BLK : (b + 1) * BLK, b * BLK : (b + 1) * BLK].astype(BF16)


def backward(q4, k4, v4, klo, khi, vlo, vhi, rb, attn_t, probs, dmix):
    out4 = jax.ShapeDtypeStruct((FR_DEV, NTILE, TILE, WID), BF16)
    halo = jax.ShapeDtypeStruct((2, RADIUS, NTILE, TILE, WID), BF16)
    halo_spec = pl.BlockSpec((2, RADIUS, 1, TILE, WID), lambda t: (0, 0, t, 0, 0))
    return pl.pallas_call(
        backward_kernel,
        grid=(NTILE,),
        in_specs=[tile_spec(FR_DEV)] * 3
        + [tile_spec(RADIUS)] * 4
        + [
            whole((WID, WID)),
            col_spec(),
            pl.BlockSpec((1, HL, 2, SPAN * TILE, 2 * TILE), lambda t: (t, 0, 0, 0, 0)),
            col_spec(),
        ],
        out_specs=[tile_spec(FR_DEV)] * 3 + [halo_spec] * 2 + [whole((HL, BLK, BLK))],
        out_shape=[out4] * 3 + [halo] * 2 + [jax.ShapeDtypeStruct((HL, BLK, BLK), BF16)],
        scratch_shapes=[pltpu.VMEM((WID, WID), F32)],
        compiler_params=params(),
        cost_estimate=pl.CostEstimate(
            flops=12 * 10**9, bytes_accessed=30 * 10**6, transcendentals=0
        ),
        name="backward",
    )(q4, k4, v4, klo, khi, vlo, vhi, rb, attn_t, probs, dmix)


def add_kernel(dk_ref, dv_ref, below_ref, above_ref, ok_ref, ov_ref):
    for which, (own, out) in enumerate(((dk_ref, ok_ref), (dv_ref, ov_ref))):
        for e in range(RADIUS):
            out[e] = (own[e].astype(F32) + below_ref[which, e].astype(F32)).astype(BF16)
            up = own[RADIUS + e].astype(F32) + above_ref[which, e].astype(F32)
            out[RADIUS + e] = up.astype(BF16)


def add_halos(dk, dv, below, above):
    halo_spec = pl.BlockSpec((2, RADIUS, 1, TILE, WID), lambda t: (0, 0, t, 0, 0))
    out4 = jax.ShapeDtypeStruct((FR_DEV, NTILE, TILE, WID), BF16)
    return pl.pallas_call(
        add_kernel,
        grid=(NTILE,),
        in_specs=[tile_spec(FR_DEV)] * 2 + [halo_spec] * 2,
        out_specs=[tile_spec(FR_DEV)] * 2,
        out_shape=[out4] * 2,
        compiler_params=params(),
        cost_estimate=pl.CostEstimate(flops=10**6, bytes_accessed=10 * 10**6, transcendentals=0),
        name="add_halos",
    )(dk, dv, below, above)


def project_kernel(perm_ref, w_ref, arr_ref, g_ref, out_ref, l_ref, acc_ref):
    t = pl.program_id(0)
    arrived = arr_ref[...]
    g = g_ref[...].reshape(COLS, WID)
    out = dot(arrived, w_ref[...], TN).astype(BF16)
    out_ref[...] = out.reshape(FR_DEV, 1, TILE, WID)
    term = dot(arrived, g)

    @pl.when(t == 0)
    def _():
        acc_ref[...] = term

    @pl.when(t > 0)
    def _():
        acc_ref[...] += term

    @pl.when(t == NTILE - 1)
    def _():
        full = dot(placer_of(perm_ref, True), acc_ref[...].astype(BF16))
        for c in range(HL):
            l_ref[c] = full[c * BLK : (c + 1) * BLK, c * BLK : (c + 1) * BLK].astype(BF16)


def project(perm, w, arrived, g4):
    return pl.pallas_call(
        project_kernel,
        grid=(NTILE,),
        in_specs=[smem(), whole((WID, WID)), col_spec(), tile_spec(FR_DEV)],
        out_specs=[tile_spec(FR_DEV), whole((HL, BLK, BLK))],
        out_shape=[
            jax.ShapeDtypeStruct((FR_DEV, NTILE, TILE, WID), BF16),
            jax.ShapeDtypeStruct((HL, BLK, BLK), BF16),
        ],
        scratch_shapes=[pltpu.VMEM((WID, WID), F32)],
        compiler_params=params(),
        cost_estimate=pl.CostEstimate(flops=10**9, bytes_accessed=6 * 10**6, transcendentals=0),
        name="project",
    )(perm, w, arrived, g4)


def tm_sum(x, norm):
    count = lax.axis_size("tm")

    def moved(y, to):
        return lax.ppermute(y, "tm", [(i, to(i)) for i in range(count)]).astype(F32)

    def along_x(by):
        return lambda i: (i // 8) * 8 + (i % 8 + 2 * by) % 8

    x = (x.astype(F32) + moved(x, lambda i: i ^ 1)).astype(BF16)
    one, two, three = moved(x, along_x(1)), moved(x, along_x(2)), moved(x, along_x(3))
    x = ((x.astype(F32) + two) + (one + three)).astype(BF16)
    x = x.astype(F32) + moved(x, lambda i: i ^ 8)
    return x * norm


def on_device(queries, keys, values, right_blocks, left_blocks, block_perm, reach, grad_out):
    rows, width = queries.shape
    count = lax.axis_size("tm")
    n_head = lax.axis_size("head")
    up = [(i, (i + 1) % count) for i in range(count)]
    down = [((i + 1) % count, i) for i in range(count)]
    shape4 = (FR_DEV, NTILE, TILE, width)
    half = (RADIUS, NTILE, TILE, width)
    q4, k4, v4, g4 = (x.reshape(shape4) for x in (queries, keys, values, grad_out))
    cut = RADIUS * NTILE * TILE
    klo = lax.ppermute(keys[rows - cut :], "tm", up).reshape(half)
    khi = lax.ppermute(keys[:cut], "tm", down).reshape(half)
    vlo = lax.ppermute(values[rows - cut :], "tm", up).reshape(half)
    vhi = lax.ppermute(values[:cut], "tm", down).reshape(half)

    w, rb, d_arrived = prep(block_perm, left_blocks, right_blocks, g4)

    def exchange(x):
        y = lax.all_to_all(
            x.reshape(n_head, width // n_head, rows), "head", split_axis=0, concat_axis=0, tiled=True
        )
        return y.reshape(width, rows)

    dmix = exchange(d_arrived)
    attn_t, probs, mixed = forward(reach, q4, k4, v4, klo, khi, vlo, vhi, rb)
    arrived = exchange(mixed)
    dq, dk, dv, lo, hi, right_term = backward(
        q4, k4, v4, klo, khi, vlo, vhi, rb, attn_t, probs, dmix
    )
    below = lax.ppermute(hi, "tm", up)
    above = lax.ppermute(lo, "tm", down)
    projected, left_term = project(block_perm, w, arrived, g4)
    dk, dv = add_halos(dk, dv, below, above)
    norm = float(rows * count) ** (-0.5)
    d_right = tm_sum(right_term, norm)
    d_left = tm_sum(left_term, norm)
    flat = (rows, width)
    return (
        projected.reshape(flat),
        dq.reshape(flat),
        dk.reshape(flat),
        dv.reshape(flat),
        d_right,
        d_left,
    )


def solution(mesh):
    in_specs = (
        P("tm", "head"),
        P("tm", "head"),
        P("tm", "head"),
        P("head", None, None),
        P("head", None, None),
        P(),
        P(),
        P("tm", "head"),
    )
    out_specs = (
        P("tm", "head"),
        P("tm", "head"),
        P("tm", "head"),
        P("tm", "head"),
        P("head", None, None),
        P("head", None, None),
    )
    return jax.shard_map(
        on_device, mesh=mesh, in_specs=in_specs, out_specs=out_specs, check_vma=False
    )
```

time: 390 us -> 131 us (0.34); the launches traced: 383 us -> 130 us
  local copies, waits for them, and re-layouts: 106 us -> 7.43 us
  matrix products: 74.1 us -> 0 us
  waiting for transfers between devices: 93.5 us -> 29 us
  other arithmetic: 55.6 us -> 2.47 us
  Pallas kernels: 0 us -> 52.9 us
  between operations: 14.6 us -> 0.73 us
    psum x1 -> x0, waiting for transfers between devices: 93.4 us -> none  [on_device(): lax.psum(right_term.astype(jnp.bfloat16), 'tm').astype(jnp.float32)]
    dot_general x35 -> x0, matrix products: 73.5 us -> none  [the longest x4 12.9 us: attend(): jnp.einsum('hqk,hkd->hqd', probs, v_rows, preferred_element_type=jnp.floa...]
    pallas_call x0 -> x5, Pallas kernels: none -> 52.9 us  [the longest x1 18.5 us: forward(): pl.pallas_call(forward_kernel, grid=(NTILE,), in_specs=[smem()] + [tile_s...]
    reshape x11 -> x0, local copies, waits for them, and re-layouts: 29.7 us -> none  [the longest x1 15.1 us: on_device(): kv_grads = kv_tiles.reshape(NTILE, 2, local_heads, span, TILE, BLK)]
    ppermute x4 -> x16, waiting for transfers between devices: 0.01 us -> 29 us  [the longest x10 19.2 us: moved(): return lax.ppermute(y, 'tm', [(i, to(i)) for i in range(count)]).astype(F32)]
    unnamed x40 -> x14, local copies, waits for them, and re-layouts: 29.9 us -> 4.6 us
    dynamic_slice x21 -> x0, local copies, waits for them, and re-layouts: 20.7 us -> none  [the longest x16 20.6 us: on_device(): attn_tiles, lse_tiles = lax.map(forward_tile, (q_tiles, k_ext, v_ext))]
    another operation x2 -> x0, other arithmetic: 13.9 us -> none
  transfers between devices with their start and end apart: 7 -> 18, of which waited for: 1 -> 5; matrix products, arithmetic and copies ran while one was open for 56% -> 2% of each run, Pallas kernels for 0% -> 37%
where the time goes in v1:
time: 131 us; the launch traced here: 130 us
  Pallas kernels  52.9 us (40%)
  starting transfers between devices  37.7 us (29%)
  waiting for transfers between devices  29 us (22%)
  local copies, waits for them, and re-layouts  7.43 us (6%)
  other arithmetic  2.47 us (2%)
    ppermute x10, waiting for transfers between devices, moved(): return lax.ppermute(y, 'tm', [(i, to(i)) for i in range(count)]).astype(F32)  19.2 us
    pallas_call x1, Pallas kernels, forward(): pl.pallas_call(forward_kernel, grid=(NTILE,), in_specs=[smem()] + [tile_s...  18.5 us
    pallas_call x1, Pallas kernels, backward(): pl.pallas_call(backward_kernel, grid=(NTILE,), in_specs=[tile_spec(FR_DEV...  18.3 us
    all_to_all x2, starting transfers between devices, exchange(): lax.all_to_all(x.reshape(n_head, width // n_head, rows), 'head', split_ax...  15.6 us
    ppermute x10, starting transfers between devices, moved(): return lax.ppermute(y, 'tm', [(i, to(i)) for i in range(count)]).astype(F32)  10.4 us
    ppermute x1, waiting for transfers between devices, on_device(): vlo = lax.ppermute(values[rows - cut:], 'tm', up).reshape(half)  9.77 us
    pallas_call x1, Pallas kernels, project(): pl.pallas_call(project_kernel, grid=(NTILE,), in_specs=[smem(), whole((WI...  6.14 us
    pallas_call x1, Pallas kernels, add_halos(): pl.pallas_call(add_kernel, grid=(NTILE,), in_specs=[tile_spec(FR_DEV)] *...  5.08 us
  transfers between devices with their start and end apart: 18, of which 5 were waited for; matrix products, arithmetic and copies ran while one was open for 2% of the time, Pallas kernels for 37%

profile of v1, /device:TPU:16, one launch (start us, length us, event | category | flops | bytes accessed | tf_op | source)
XLA Modules:
  0.0 130.3 jit_solution(18340039270699134578)
XLA Ops:
  0.6 2.7 %fusion.1 = (bf16[1024,384]{1,0:T(8,128)(2,1)}, bf16[1024,384]{1,0:T(8,128)(2,1)}) fusion(bf16[2048,384]{1,0:T(8,128)(2,1)} %param.9), kind=kLoop, calls=%fused_computation.7 | loop fusion | bytes 3145728 | tf_op jit(solution)/shard_map/slice | solution.py:361
  3.3 0.0 collective-permute-start
  3.3 3.9 %collective-permute-start.1 = (bf16[1024,384]{1,0:T(8,128)(2,1)}, bf16[1024,384]{1,0:T(8,128)(2,1)}, u32[]{:S(2)}, u32[]{:S(2)}) collective-permute-start(bf16[1024,384]{1,0:T(8,128)(2,1)} %get-tuple-element.40), channel_id=1, source_target_pairs={{8,0},{16,8},{24,16},{32,24},{40,32},{48,40},{56,48},{64,56},{72,6... | collective-permute-start | bytes 2359304 | tf_op jit(solution)/shard_map/ppermute | solution.py:361
  7.2 4.9 %prep.1 = (bf16[384,384]{1,0:T(8,128)(2,1)}, bf16[384,384]{1,0:T(8,128)(2,1)}, bf16[384,2048]{1,0:T(8,128)(2,1)}) custom-call(s32[24]{0:T(128)} %perm_ref.3, bf16[3,128,128]{2,1,0:T(8,128)(2,1)} %left_ref.1, bf16[3,128,128]{2,1,0:T(8,128)(2,1)} %right_ref.1, bf16[4,4,128,384]{3,2,1,0:T(8,128)(2,1)} %bitcast.26), custom_call_target="tpu_custom_call" | custom-call | flops 1000000000 | bytes 4000000 | tf_op jit(solution)/shard_map/prep/pallas_call | solution.py:99
  12.1 0.0 copy-start
  12.1 8.4 %all-to-all-start.1 = ((bf16[8,48,2048]{2,1,0:T(8,128)(2,1)}), bf16[8,48,2048]{2,1,0:T(8,128)(2,1)S(1)}, u32[]{:S(2)}, u32[]{:S(2)}) async-start(bf16[8,48,2048]{2,1,0:T(8,128)(2,1)} %bitcast.22), calls=%async_computation.1 | async-start | bytes 3145728 | tf_op jit(solution)/shard_map/all_to_all | solution.py:368
  20.5 0.0 copy-done
  20.5 0.2 fusion
  20.6 0.1 collective-permute-start.2
  20.7 3.8 %collective-permute-start.3 = (bf16[1024,384]{1,0:T(8,128)(2,1)S(1)}, bf16[1024,384]{1,0:T(8,128)(2,1)S(1)}, u32[]{:S(2)}, u32[]{:S(2)}) collective-permute-start(bf16[1024,384]{1,0:T(8,128)(2,1)S(1)} %get-tuple-element.38), channel_id=1, source_target_pairs={{8,0},{16,8},{24,16},{32,24},{40,32},{48,40},{56,48},{64,56},{72,6... | collective-permute-start | bytes 2359304 | tf_op jit(solution)/shard_map/ppermute | solution.py:363
  24.6 0.0 collective-permute-done
  24.6 0.0 collective-permute-done.1
  24.6 9.8 %collective-permute-done.2 = bf16[1024,384]{1,0:T(8,128)(2,1)S(1)} collective-permute-done((bf16[1024,384]{1,0:T(8,128)(2,1)S(1)}, bf16[1024,384]{1,0:T(8,128)(2,1)S(1)}, u32[]{:S(2)}, u32[]{:S(2)}) %collective-permute-start.2) | collective-permute-done | bytes 786464 | tf_op jit(solution)/shard_map/ppermute | solution.py:362
  34.3 0.0 copy-start.5
  34.3 0.0 collective-permute-done.3
  34.3 0.0 copy-start.6
  34.3 0.9 copy-done.5
  35.2 0.3 copy-done.6
  35.5 18.5 %forward.1 = (bf16[384,2048]{1,0:T(8,128)(2,1)}, bf16[4,3,2,768,256]{4,3,2,1,0:T(8,128)(2,1)}, bf16[384,2048]{1,0:T(8,128)(2,1)}) custom-call(s32[24]{0:T(128)} %reach_ref.1, bf16[4,4,128,384]{3,2,1,0:T(8,128)(2,1)} %bitcast.24, bf16[4,4,128,384]{3,2,1,0:T(8,128)(2,1)} %bitcast.16, bf16[4,4,128,384]{3,2,1,0:T(8,128)(2,1)} %bitcast.18, ...), custom_call_target="tpu_custom_call" | custom-call | flops 6000000000 | bytes 20000000 | tf_op jit(solution)/shard_map/forward/pallas_call | solution.py:169
  54.0 0.0 all-to-all-done.1
  54.0 0.0 copy-start.1
  54.0 1.1 copy-done.1
  55.2 7.2 %all-to-all-start = ((bf16[8,48,2048]{2,1,0:T(8,128)(2,1)}), bf16[8,48,2048]{2,1,0:T(8,128)(2,1)S(1)}, u32[]{:S(2)}, u32[]{:S(2)}) async-start(bf16[8,48,2048]{2,1,0:T(8,128)(2,1)} %bitcast.23), calls=%async_computation | async-start | bytes 3145728 | tf_op jit(solution)/shard_map/all_to_all | solution.py:368
  62.4 18.3 %backward.1 = (bf16[4,4,128,384]{3,2,1,0:T(8,128)(2,1)}, bf16[4,4,128,384]{3,2,1,0:T(8,128)(2,1)}, bf16[4,4,128,384]{3,2,1,0:T(8,128)(2,1)}, bf16[2,2,4,128,384]...) custom-call(bf16[4,4,128,384]{3,2,1,0:T(8,128)(2,1)} %bitcast.25, ...), custom_call_target="tpu_custom_call" | custom-call | flops 12000000000 | bytes 30000000 | tf_op jit(solution)/shard_map/backward/pallas_call | solution.py:249
  80.7 0.1 collective-permute-start.4
  80.7 3.8 %collective-permute-start.5 = (bf16[2,2,4,128,384]{4,3,2,1,0:T(8,128)(2,1)}, bf16[2,2,4,128,384]{4,3,2,1,0:T(8,128)(2,1)}, u32[]{:S(2)}, u32[]{:S(2)}) collective-permute-start(bf16[2,2,4,128,384]{4,3,2,1,0:T(8,128)(2,1)} %get-tuple-element.33), channel_id=1, source_target_pairs={{8,0},{16,8},{24,16},{32,24},{40,32},{48,40},{56,48},{64,56},{72,6... | collective-permute-start | bytes 4718600 | tf_op jit(solution)/shard_map/ppermute | solution.py:380
  84.6 0.0 collective-permute-start.6
  84.6 0.0 all-to-all-done
  84.6 0.0 copy-start.2
  84.6 1.1 copy-done.2
  85.7 0.0 copy-start.4
  85.7 6.1 %project.1 = (bf16[4,4,128,384]{3,2,1,0:T(8,128)(2,1)}, bf16[3,128,128]{2,1,0:T(8,128)(2,1)}) custom-call(s32[24]{0:T(128)} %perm_ref.3, bf16[384,384]{1,0:T(8,128)(2,1)} %get-tuple-element.22.w_ref, bf16[384,2048]{1,0:T(8,128)(2,1)} %bitcast.21, bf16[4,4,128,384]{3,2,1,0:T(8,128)(2,1)} %bitcast.27), custom_call_target="tpu_custom_call" | custom-call | flops 1000000000 | bytes 6000000 | tf_op jit(solution)/shard_map/project/pallas_call | solution.py:318
  91.9 0.5 collective-permute-start.11
  92.4 0.0 collective-permute-done.6
  92.4 0.0 copy-done.4
  92.4 0.1 collective-permute-start.9
  92.5 2.0 %collective-permute-start.8 = (bf16[3,128,128]{2,1,0:T(8,128)(2,1)S(1)}, bf16[3,128,128]{2,1,0:T(8,128)(2,1)S(1)}, u32[]{:S(2)}, u32[]{:S(2)}) collective-permute-start(bf16[3,128,128]{2,1,0:T(8,128)(2,1)S(1)} %add_convert_fusion.3), channel_id=1, source_target_pairs={{0,16},{8,24},{16,32},{24,40},{32,48},{40,56},{48,0},{56,8},{64,80... | collective-permute-start | bytes 294920 | tf_op jit(solution)/shard_map/ppermute | solution.py:338
  94.5 0.0 collective-permute-done.11
  94.5 0.0 collective-permute-start.7
  94.5 0.9 add_convert_fusion.1
  95.5 12.5 %collective-permute-done.9 = bf16[3,128,128]{2,1,0:T(8,128)(2,1)S(1)} collective-permute-done((bf16[3,128,128]{2,1,0:T(8,128)(2,1)S(1)}, bf16[3,128,128]{2,1,0:T(8,128)(2,1)S(1)}, u32[]{:S(2)}, u32[]{:S(2)}) %collective-permute-start.9) | collective-permute-done | bytes 98336 | tf_op jit(solution)/shard_map/ppermute | solution.py:338
  108.0 3.7 %collective-permute-start.14 = (bf16[3,128,128]{2,1,0:T(8,128)(2,1)S(1)}, bf16[3,128,128]{2,1,0:T(8,128)(2,1)S(1)}, u32[]{:S(2)}, u32[]{:S(2)}) collective-permute-start(bf16[3,128,128]{2,1,0:T(8,128)(2,1)S(1)} %add_convert_fusion.1), channel_id=1, source_target_pairs={{0,48},{8,56},{16,0},{24,8},{32,16},{40,24},{48,32},{56,40},{64,11... | collective-permute-start | bytes 294920 | tf_op jit(solution)/shard_map/ppermute | solution.py:338
  111.7 0.0 collective-permute-done.8
  111.7 0.0 collective-permute-start.13
  111.7 0.0 collective-permute-done.7
  111.7 1.5 %collective-permute-start.12 = (bf16[3,128,128]{2,1,0:T(8,128)(2,1)S(1)}, bf16[3,128,128]{2,1,0:T(8,128)(2,1)S(1)}, u32[]{:S(2)}, u32[]{:S(2)}) collective-permute-start(bf16[3,128,128]{2,1,0:T(8,128)(2,1)S(1)} %add_convert_fusion.1), channel_id=1, source_target_pairs={{0,32},{8,40},{16,48},{24,56},{32,0},{40,8},{48,16},{56,24},{64,96... | collective-permute-start | bytes 294920 | tf_op jit(solution)/shard_map/ppermute | solution.py:338
  113.2 0.1 add_convert_fusion.2
  113.2 0.7 collective-permute-done.14
  113.9 1.3 collective-permute-start.10
  115.2 3.4 %collective-permute-done.13 = bf16[3,128,128]{2,1,0:T(8,128)(2,1)S(1)} collective-permute-done((bf16[3,128,128]{2,1,0:T(8,128)(2,1)S(1)}, bf16[3,128,128]{2,1,0:T(8,128)(2,1)S(1)}, u32[]{:S(2)}, u32[]{:S(2)}) %collective-permute-start.13) | collective-permute-done | bytes 98336 | tf_op jit(solution)/shard_map/ppermute | solution.py:338
  118.6 0.0 collective-permute-done.12
  118.6 0.1 add_convert_fusion
  118.6 1.4 %collective-permute-start.15 = (bf16[3,128,128]{2,1,0:T(8,128)(2,1)S(1)}, bf16[3,128,128]{2,1,0:T(8,128)(2,1)S(1)}, u32[]{:S(2)}, u32[]{:S(2)}) collective-permute-start(bf16[3,128,128]{2,1,0:T(8,128)(2,1)S(1)} %add_convert_fusion), channel_id=1, source_target_pairs={{0,64},{8,72},{16,80},{24,88},{32,96},{40,104},{48,112},{56,120},{... | collective-permute-start | bytes 294920 | tf_op jit(solution)/shard_map/ppermute | solution.py:338
  120.0 0.0 collective-permute-done.10
  120.0 0.7 add_multiply_fusion.1
  120.7 2.6 %collective-permute-done.15 = bf16[3,128,128]{2,1,0:T(8,128)(2,1)S(1)} collective-permute-done((bf16[3,128,128]{2,1,0:T(8,128)(2,1)S(1)}, bf16[3,128,128]{2,1,0:T(8,128)(2,1)S(1)}, u32[]{:S(2)}, u32[]{:S(2)}) %collective-permute-start.15) | collective-permute-done | bytes 98336 | tf_op jit(solution)/shard_map/ppermute | solution.py:338
  123.3 0.7 add_multiply_fusion
  124.0 0.0 collective-permute-done.4.below_ref
  124.1 0.0 copy-start.3
  124.1 0.0 collective-permute-done.5.above_ref
  124.1 1.1 copy-done.3
  125.2 5.1 %add_halos.1 = (bf16[4,4,128,384]{3,2,1,0:T(8,128)(2,1)}, bf16[4,4,128,384]{3,2,1,0:T(8,128)(2,1)}) custom-call(bf16[4,4,128,384]{3,2,1,0:T(8,128)(2,1)} %get-tuple-element.30.dk_ref, bf16[4,4,128,384]{3,2,1,0:T(8,128)(2,1)} %get-tuple-element.31.dv_ref, bf16[2,2,4,128,384]{4,3,2,1,0:T(8,128)(2,1)} %copy-done.3, ...), custom_call_target="tpu_custom_call" | custom-call | flops 1000000 | bytes 10000000 | tf_op jit(solution)/shard_map/add_halos/pallas_call | solution.py:282
  (1 shorter events, 0.0 us)
Async XLA Ops:
  3.3 21.3 %collective-permute-start = (bf16[1024,384]{1,0:T(8,128)(2,1)}, bf16[1024,384]{1,0:T(8,128)(2,1)}, u32[]{:S(2)}, u32[]{:S(2)}) collective-permute-start(bf16[1024,384]{1,0:T(8,128)(2,1)} %get-tuple-element.41), channel_id=1, source_target_pairs={{0,8},{8,16},{16,24},{24,32},{32,40},{40,48},{48,56},{56,64},{64,7... | collective-permute-start | bytes 2359304 | tf_op jit(solution)/shard_map/ppermute | solution.py:360
  3.3 21.3 %collective-permute-start.1 = (bf16[1024,384]{1,0:T(8,128)(2,1)}, bf16[1024,384]{1,0:T(8,128)(2,1)}, u32[]{:S(2)}, u32[]{:S(2)}) collective-permute-start(bf16[1024,384]{1,0:T(8,128)(2,1)} %get-tuple-element.40), channel_id=1, source_target_pairs={{8,0},{16,8},{24,16},{32,24},{40,32},{48,40},{56,48},{64,56},{72,6... | collective-permute-start | bytes 2359304 | tf_op jit(solution)/shard_map/ppermute | solution.py:361
  12.1 8.4 %copy-start = (bf16[2048,384]{1,0:T(8,128)(2,1)S(1)}, bf16[2048,384]{1,0:T(8,128)(2,1)}, u32[]{:S(2)}) copy-start(bf16[2048,384]{1,0:T(8,128)(2,1)} %param.10) | copy-start | bytes 4718596
  12.1 42.0 %all-to-all-start.1 = ((bf16[8,48,2048]{2,1,0:T(8,128)(2,1)}), bf16[8,48,2048]{2,1,0:T(8,128)(2,1)S(1)}, u32[]{:S(2)}, u32[]{:S(2)}) async-start(bf16[8,48,2048]{2,1,0:T(8,128)(2,1)} %bitcast.22), calls=%async_computation.1 | async-start | bytes 3145728 | tf_op jit(solution)/shard_map/all_to_all | solution.py:368
  20.6 13.7 %collective-permute-start.2 = (bf16[1024,384]{1,0:T(8,128)(2,1)S(1)}, bf16[1024,384]{1,0:T(8,128)(2,1)S(1)}, u32[]{:S(2)}, u32[]{:S(2)}) collective-permute-start(bf16[1024,384]{1,0:T(8,128)(2,1)S(1)} %get-tuple-element.39), channel_id=1, source_target_pairs={{0,8},{8,16},{16,24},{24,32},{32,40},{40,48},{48,56},{56,64},{64,7... | collective-permute-start | bytes 2359304 | tf_op jit(solution)/shard_map/ppermute | solution.py:362
  20.7 13.6 %collective-permute-start.3 = (bf16[1024,384]{1,0:T(8,128)(2,1)S(1)}, bf16[1024,384]{1,0:T(8,128)(2,1)S(1)}, u32[]{:S(2)}, u32[]{:S(2)}) collective-permute-start(bf16[1024,384]{1,0:T(8,128)(2,1)S(1)} %get-tuple-element.38), channel_id=1, source_target_pairs={{8,0},{16,8},{24,16},{32,24},{40,32},{48,40},{56,48},{64,56},{72,6... | collective-permute-start | bytes 2359304 | tf_op jit(solution)/shard_map/ppermute | solution.py:363
  34.3 0.9 copy-start.5
  34.3 1.2 copy-start.6
  54.0 1.1 copy-start.1
  55.2 29.4 %all-to-all-start = ((bf16[8,48,2048]{2,1,0:T(8,128)(2,1)}), bf16[8,48,2048]{2,1,0:T(8,128)(2,1)S(1)}, u32[]{:S(2)}, u32[]{:S(2)}) async-start(bf16[8,48,2048]{2,1,0:T(8,128)(2,1)} %bitcast.23), calls=%async_computation | async-start | bytes 3145728 | tf_op jit(solution)/shard_map/all_to_all | solution.py:368
  80.7 43.4 %collective-permute-start.4 = (bf16[2,2,4,128,384]{4,3,2,1,0:T(8,128)(2,1)}, bf16[2,2,4,128,384]{4,3,2,1,0:T(8,128)(2,1)S(1)}, u32[]{:S(2)}, u32[]{:S(2)}) collective-permute-start(bf16[2,2,4,128,384]{4,3,2,1,0:T(8,128)(2,1)} %get-tuple-element.32), channel_id=1, source_target_pairs={{0,8},{8,16},{16,24},{24,32},{32,40},{40,48},{48,56},{56,64},{64,7... | collective-permute-start | bytes 4718600 | tf_op jit(solution)/shard_map/ppermute | solution.py:379
  80.7 43.3 %collective-permute-start.5 = (bf16[2,2,4,128,384]{4,3,2,1,0:T(8,128)(2,1)}, bf16[2,2,4,128,384]{4,3,2,1,0:T(8,128)(2,1)}, u32[]{:S(2)}, u32[]{:S(2)}) collective-permute-start(bf16[2,2,4,128,384]{4,3,2,1,0:T(8,128)(2,1)} %get-tuple-element.33), channel_id=1, source_target_pairs={{8,0},{16,8},{24,16},{32,24},{40,32},{48,40},{56,48},{64,56},{72,6... | collective-permute-start | bytes 4718600 | tf_op jit(solution)/shard_map/ppermute | solution.py:380
  84.6 7.8 %collective-permute-start.6 = (bf16[3,128,128]{2,1,0:T(8,128)(2,1)}, bf16[3,128,128]{2,1,0:T(8,128)(2,1)S(1)}, u32[]{:S(2)}, u32[]{:S(2)}) collective-permute-start(bf16[3,128,128]{2,1,0:T(8,128)(2,1)} %get-tuple-element.36), channel_id=1, source_target_pairs={{0,8},{8,0},{16,24},{24,16},{32,40},{40,32},{48,56},{56,48},{64,72... | collective-permute-start | bytes 294920 | tf_op jit(solution)/shard_map/ppermute | solution.py:338
  84.6 1.1 copy-start.2
  85.7 6.7 %copy-start.4 = (bf16[3,128,128]{2,1,0:T(8,128)(2,1)S(1)}, bf16[3,128,128]{2,1,0:T(8,128)(2,1)}, u32[]{:S(2)}) copy-start(bf16[3,128,128]{2,1,0:T(8,128)(2,1)} %get-tuple-element.36) | copy-start | bytes 294916
  91.9 2.6 %collective-permute-start.11 = (bf16[3,128,128]{2,1,0:T(8,128)(2,1)}, bf16[3,128,128]{2,1,0:T(8,128)(2,1)S(1)}, u32[]{:S(2)}, u32[]{:S(2)}) collective-permute-start(bf16[3,128,128]{2,1,0:T(8,128)(2,1)} %get-tuple-element.37), channel_id=1, source_target_pairs={{0,8},{8,0},{16,24},{24,16},{32,40},{40,32},{48,56},{56,48},{64,72... | collective-permute-start | bytes 294920 | tf_op jit(solution)/shard_map/ppermute | solution.py:338
  92.4 15.6 %collective-permute-start.9 = (bf16[3,128,128]{2,1,0:T(8,128)(2,1)S(1)}, bf16[3,128,128]{2,1,0:T(8,128)(2,1)S(1)}, u32[]{:S(2)}, u32[]{:S(2)}) collective-permute-start(bf16[3,128,128]{2,1,0:T(8,128)(2,1)S(1)} %add_convert_fusion.3), channel_id=1, source_target_pairs={{0,48},{8,56},{16,0},{24,8},{32,16},{40,24},{48,32},{56,40},{64,11... | collective-permute-start | bytes 294920 | tf_op jit(solution)/shard_map/ppermute | solution.py:338
  92.5 19.2 %collective-permute-start.8 = (bf16[3,128,128]{2,1,0:T(8,128)(2,1)S(1)}, bf16[3,128,128]{2,1,0:T(8,128)(2,1)S(1)}, u32[]{:S(2)}, u32[]{:S(2)}) collective-permute-start(bf16[3,128,128]{2,1,0:T(8,128)(2,1)S(1)} %add_convert_fusion.3), channel_id=1, source_target_pairs={{0,16},{8,24},{16,32},{24,40},{32,48},{40,56},{48,0},{56,8},{64,80... | collective-permute-start | bytes 294920 | tf_op jit(solution)/shard_map/ppermute | solution.py:338
  94.5 17.2 %collective-permute-start.7 = (bf16[3,128,128]{2,1,0:T(8,128)(2,1)S(1)}, bf16[3,128,128]{2,1,0:T(8,128)(2,1)S(1)}, u32[]{:S(2)}, u32[]{:S(2)}) collective-permute-start(bf16[3,128,128]{2,1,0:T(8,128)(2,1)S(1)} %add_convert_fusion.3), channel_id=1, source_target_pairs={{0,32},{8,40},{16,48},{24,56},{32,0},{40,8},{48,16},{56,24},{64,96... | collective-permute-start | bytes 294920 | tf_op jit(solution)/shard_map/ppermute | solution.py:338
  108.0 5.9 %collective-permute-start.14 = (bf16[3,128,128]{2,1,0:T(8,128)(2,1)S(1)}, bf16[3,128,128]{2,1,0:T(8,128)(2,1)S(1)}, u32[]{:S(2)}, u32[]{:S(2)}) collective-permute-start(bf16[3,128,128]{2,1,0:T(8,128)(2,1)S(1)} %add_convert_fusion.1), channel_id=1, source_target_pairs={{0,48},{8,56},{16,0},{24,8},{32,16},{40,24},{48,32},{56,40},{64,11... | collective-permute-start | bytes 294920 | tf_op jit(solution)/shard_map/ppermute | solution.py:338
  111.7 6.9 %collective-permute-start.13 = (bf16[3,128,128]{2,1,0:T(8,128)(2,1)S(1)}, bf16[3,128,128]{2,1,0:T(8,128)(2,1)S(1)}, u32[]{:S(2)}, u32[]{:S(2)}) collective-permute-start(bf16[3,128,128]{2,1,0:T(8,128)(2,1)S(1)} %add_convert_fusion.1), channel_id=1, source_target_pairs={{0,16},{8,24},{16,32},{24,40},{32,48},{40,56},{48,0},{56,8},{64,80... | collective-permute-start | bytes 294920 | tf_op jit(solution)/shard_map/ppermute | solution.py:338
  111.7 6.9 %collective-permute-start.12 = (bf16[3,128,128]{2,1,0:T(8,128)(2,1)S(1)}, bf16[3,128,128]{2,1,0:T(8,128)(2,1)S(1)}, u32[]{:S(2)}, u32[]{:S(2)}) collective-permute-start(bf16[3,128,128]{2,1,0:T(8,128)(2,1)S(1)} %add_convert_fusion.1), channel_id=1, source_target_pairs={{0,32},{8,40},{16,48},{24,56},{32,0},{40,8},{48,16},{56,24},{64,96... | collective-permute-start | bytes 294920 | tf_op jit(solution)/shard_map/ppermute | solution.py:338
  113.9 6.1 %collective-permute-start.10 = (bf16[3,128,128]{2,1,0:T(8,128)(2,1)S(1)}, bf16[3,128,128]{2,1,0:T(8,128)(2,1)S(1)}, u32[]{:S(2)}, u32[]{:S(2)}) collective-permute-start(bf16[3,128,128]{2,1,0:T(8,128)(2,1)S(1)} %add_convert_fusion.2), channel_id=1, source_target_pairs={{0,64},{8,72},{16,80},{24,88},{32,96},{40,104},{48,112},{56,120},{... | collective-permute-start | bytes 294920 | tf_op jit(solution)/shard_map/ppermute | solution.py:338
  118.6 4.7 %collective-permute-start.15 = (bf16[3,128,128]{2,1,0:T(8,128)(2,1)S(1)}, bf16[3,128,128]{2,1,0:T(8,128)(2,1)S(1)}, u32[]{:S(2)}, u32[]{:S(2)}) collective-permute-start(bf16[3,128,128]{2,1,0:T(8,128)(2,1)S(1)} %add_convert_fusion), channel_id=1, source_target_pairs={{0,64},{8,72},{16,80},{24,88},{32,96},{40,104},{48,112},{56,120},{... | collective-permute-start | bytes 294920 | tf_op jit(solution)/shard_map/ppermute | solution.py:338
  124.1 1.1 copy-start.3

commit v2 on v1

v2 whole, which is shorter than its diff:
```python
import functools

import jax
import jax.numpy as jnp
from jax import lax
from jax.experimental import pallas as pl
from jax.experimental.pallas import tpu as pltpu
from jax.sharding import PartitionSpec as P

NB = 24
BLK = 128
TILE = 128
RADIUS = 2
FR_DEV = 4
NTILE = 4
NF = 64
HL = 3
WID = HL * BLK
ROWS = FR_DEV * NTILE * TILE
COLS = FR_DEV * TILE
PIECE = 16
SCALE = BLK ** (-0.5)
LOG2E = 1.4426950408889634
NEG = -1e30
F32 = jnp.float32
BF16 = jnp.bfloat16
VMEM = 56 * 1024 * 1024

NN = (((1,), (0,)), ((), ()))
NT = (((1,), (1,)), ((), ()))
TN = (((0,), (0,)), ((), ()))


def dot(a, b, dims=NN):
    return lax.dot_general(a, b, dims, preferred_element_type=F32)


def params():
    return pltpu.CompilerParams(
        vmem_limit_bytes=VMEM, dimension_semantics=("arbitrary",)
    )


def placer_of(perm_ref, flip):
    shape = (WID, 1) if flip else (1, WID)
    col = lax.broadcasted_iota(jnp.int32, shape, 0 if flip else 1)
    block = lax.rem(col, NB)
    lane = lax.div(col, NB)
    source = jnp.zeros(shape, jnp.int32)
    for b in range(NB):
        source = jnp.where(block == b, perm_ref[b] * PIECE, source)
    source = source + lane
    row = lax.broadcasted_iota(jnp.int32, (WID, WID), 1 if flip else 0)
    return jnp.where(row == source, 1.0, 0.0).astype(BF16)


def block_diag(blocks):
    rows = []
    for c in range(HL):
        parts = [blocks[c] if d == c else jnp.zeros((BLK, BLK), BF16) for d in range(HL)]
        rows.append(jnp.concatenate(parts, axis=1))
    return jnp.concatenate(rows, axis=0)


def piece_order():
    col = lax.broadcasted_iota(jnp.int32, (1, WID), 1)
    s = lax.div(col, HL * PIECE)
    rest = col - s * (HL * PIECE)
    want = (rest // PIECE) * BLK + s * PIECE + rest % PIECE
    row = lax.broadcasted_iota(jnp.int32, (WID, WID), 0)
    return jnp.where(row == want, 1.0, 0.0).astype(BF16)


def piece_order_t():
    row = lax.broadcasted_iota(jnp.int32, (WID, 1), 0)
    s = lax.div(row, HL * PIECE)
    rest = row - s * (HL * PIECE)
    want = (rest // PIECE) * BLK + s * PIECE + rest % PIECE
    col = lax.broadcasted_iota(jnp.int32, (WID, WID), 1)
    return jnp.where(col == want, 1.0, 0.0).astype(BF16)


def eye(n):
    row = lax.broadcasted_iota(jnp.int32, (n, n), 0)
    col = lax.broadcasted_iota(jnp.int32, (n, n), 1)
    return jnp.where(row == col, 1.0, 0.0).astype(BF16)


def turned(x):
    return dot(eye(x.shape[1]), x, NT).astype(BF16)


def gate(x, *after):
    return pl.pallas_call(
        lambda *refs: None,
        in_specs=[pl.BlockSpec(memory_space=pl.ANY)] * (1 + len(after)),
        out_specs=pl.BlockSpec(memory_space=pl.ANY),
        out_shape=jax.ShapeDtypeStruct(x.shape, x.dtype),
        input_output_aliases={0: 0},
        compiler_params=pltpu.CompilerParams(vmem_limit_bytes=VMEM),
        name="gate",
    )(x, *after)


def whole(shape):
    return pl.BlockSpec(shape, lambda t: (0,) * len(shape))


def smem():
    return pl.BlockSpec(memory_space=pltpu.SMEM)


def tile_spec(frames, first=0):
    return pl.BlockSpec((frames, 1, TILE, WID), lambda t: (0, t + first, 0, 0))


def pair_spec():
    return pl.BlockSpec((2, RADIUS, 1, TILE, WID), lambda t: (0, 0, t, 0, 0))


def col_spec(first=0):
    return pl.BlockSpec((WID, COLS), lambda t: (0, t + first))


SPAN = 6
HALO = (2, RADIUS, NTILE, TILE, WID)
OUT4 = (FR_DEV, NTILE, TILE, WID)


def prep_kernel(perm_ref, left_ref, right_ref, g_ref, w_ref, rb_ref, rbt_ref, da_ref):
    @pl.when(pl.program_id(0) == 0)
    def _():
        w_ref[...] = dot(placer_of(perm_ref, False), block_diag(left_ref[...])).astype(BF16)
        rb = dot(block_diag(right_ref[...]), piece_order()).astype(BF16)
        rb_ref[...] = rb
        rbt_ref[...] = turned(rb)

    g = g_ref[...].reshape(COLS, WID)
    da_ref[...] = dot(w_ref[...], g, NT).astype(BF16)


def prep(perm, left, right, g4):
    square = jax.ShapeDtypeStruct((WID, WID), BF16)
    return pl.pallas_call(
        prep_kernel,
        grid=(NTILE,),
        in_specs=[smem(), whole((HL, BLK, BLK)), whole((HL, BLK, BLK)), tile_spec(FR_DEV)],
        out_specs=[whole((WID, WID))] * 3 + [col_spec()],
        out_shape=[square] * 3 + [jax.ShapeDtypeStruct((WID, ROWS), BF16)],
        compiler_params=params(),
        cost_estimate=pl.CostEstimate(flops=10**9, bytes_accessed=4 * 10**6, transcendentals=0),
        name="prep",
    )(perm, left, right, g4)


def ext_rows(lo, own, hi, which, h):
    cols = slice(h * BLK, (h + 1) * BLK)
    parts = [lo[which][e, 0, :, cols] for e in range(RADIUS)]
    parts += [own[e, 0, :, cols] for e in range(FR_DEV)]
    parts += [hi[which][e, 0, :, cols] for e in range(RADIUS)]
    return jnp.concatenate(parts, axis=0)


def ext_span(pair):
    return slice(2 * pair * TILE, (2 * pair + SPAN) * TILE)


UNITS = [(h, pair) for h in range(HL) for pair in range(2)]


def forward_kernel(
    reach_ref, q_ref, k_ref, v_ref, klo, khi, vlo, vhi, rbt_ref, at_ref, p_ref, inv_ref, mix_ref
):
    lo, hi = (klo, vlo), (khi, vhi)
    base = lax.axis_index("tm") * FR_DEV
    head0 = lax.axis_index("head") * HL
    ones = jnp.ones((16, (FR_DEV + 2 * RADIUS) * TILE), BF16)
    vts = {}

    def scores(h, pair):
        cols = slice(h * BLK, (h + 1) * BLK)
        q = q_ref[2 * pair : 2 * pair + 2, 0, :, cols].reshape(2 * TILE, BLK)
        return dot(ext_rows(lo, k_ref, hi, 0, h)[ext_span(pair)], q, NT)

    s_next = scores(*UNITS[0])
    for index, (h, pair) in enumerate(UNITS):
        s = s_next
        if index + 1 < len(UNITS):
            s_next = scores(*UNITS[index + 1])
        if pair == 0:
            vts[h] = jnp.concatenate([ext_rows(lo, v_ref, hi, 1, h).T, ones], axis=0)
        reach = reach_ref[head0 + h]
        f0 = 2 * pair
        halves = []
        for a in range(2):
            parts, rows = [], []
            for j in range(5):
                frame = base + f0 + a + j - RADIUS
                ok = (abs(j - RADIUS) <= reach) & (frame >= 0) & (frame < NF)
                e = a + j
                x = s[e * TILE : (e + 1) * TILE, a * TILE : (a + 1) * TILE]
                bias = jnp.where(ok, 0.0, NEG)
                parts.append((x, bias))
                rows.append(jnp.max(x, axis=0, keepdims=True) * (SCALE * LOG2E) + bias)
            top = functools.reduce(jnp.maximum, rows)
            x = [jnp.exp2(x * (SCALE * LOG2E) + (bias - top)).astype(BF16) for x, bias in parts]
            zero = [jnp.zeros((TILE, TILE), BF16)]
            halves.append(jnp.concatenate(x + zero if a == 0 else zero + x, axis=0))
        p = jnp.concatenate(halves, axis=1)
        p_ref[0, h, pair] = p
        out = dot(vts[h][:, ext_span(pair)], p)
        inv = 1.0 / out[BLK : BLK + 1]
        lanes = slice(f0 * TILE, (f0 + 2) * TILE)
        inv_ref[0, h : h + 1, lanes] = inv
        at_ref[h * BLK : (h + 1) * BLK, lanes] = (out[:BLK] * inv).astype(BF16)
    mix_ref[...] = dot(rbt_ref[...], at_ref[...]).astype(BF16)


def p_spec():
    return pl.BlockSpec((1, HL, 2, SPAN * TILE, 2 * TILE), lambda t: (t, 0, 0, 0, 0))


def inv_spec():
    return pl.BlockSpec((1, 8, COLS), lambda t: (t, 0, 0))


def forward(reach, q4, k4, v4, halos, rbt):
    cols = jax.ShapeDtypeStruct((WID, ROWS), BF16)
    return pl.pallas_call(
        forward_kernel,
        grid=(NTILE,),
        in_specs=[smem()]
        + [tile_spec(FR_DEV)] * 3
        + [tile_spec(RADIUS)] * 4
        + [whole((WID, WID))],
        out_specs=[col_spec(), p_spec(), inv_spec(), col_spec()],
        out_shape=[
            cols,
            jax.ShapeDtypeStruct((NTILE, HL, 2, SPAN * TILE, 2 * TILE), BF16),
            jax.ShapeDtypeStruct((NTILE, 8, COLS), F32),
            cols,
        ],
        compiler_params=params(),
        cost_estimate=pl.CostEstimate(
            flops=6 * 10**9, bytes_accessed=20 * 10**6, transcendentals=4 * 10**6
        ),
        name="forward",
    )(reach, q4, k4, v4, *halos, rbt)


def backward_kernel(
    q_ref, k_ref, v_ref, klo, khi, vlo, vhi, rb_ref, at_ref, p_ref, inv_ref, dm_ref,
    dq_ref, dk_ref, dv_ref, lo_ref, hi_ref, r_ref, acc_ref,
):
    lo, hi = (klo, vlo), (khi, vhi)
    t = pl.program_id(0)
    term = dot(at_ref[...], dm_ref[...], NT)

    @pl.when(t == 0)
    def _():
        acc_ref[...] = term

    @pl.when(t > 0)
    def _():
        acc_ref[...] += term

    dat_all = dot(rb_ref[...], dm_ref[...])

    def start(h, pair):
        cols = slice(h * BLK, (h + 1) * BLK)
        lanes = slice(2 * pair * TILE, (2 * pair + 2) * TILE)
        d_t = (dat_all[cols, lanes] * inv_ref[0, h : h + 1, lanes]).astype(BF16)
        delta = jnp.sum(d_t.astype(F32) * at_ref[cols, lanes].astype(F32), axis=0, keepdims=True)
        return d_t, delta, dot(ext_rows(lo, v_ref, hi, 1, h)[ext_span(pair)], d_t)

    coming = start(*UNITS[0])
    for h in range(HL):
        cols = slice(h * BLK, (h + 1) * BLK)
        k = ext_rows(lo, k_ref, hi, 0, h)
        dks, dvs = [], []
        for pair in range(2):
            d_t, delta, dp = coming
            index = 2 * h + pair + 1
            if index < len(UNITS):
                coming = start(*UNITS[index])
            f0 = 2 * pair
            q = q_ref[f0 : f0 + 2, 0, :, cols].reshape(2 * TILE, BLK)
            p = p_ref[0, h, pair]
            dvs.append(dot(p, d_t, NT))
            grads = (p.astype(F32) * (dp - delta)).astype(BF16)
            dks.append(dot(grads, q) * SCALE)
            dq = (dot(grads, k[ext_span(pair)], TN) * SCALE).astype(BF16)
            dq_ref[f0 : f0 + 2, 0, :, cols] = dq.reshape(2, TILE, BLK)
        for which, (low, high) in enumerate((dks, dvs)):
            own_ref = dk_ref if which == 0 else dv_ref
            for e in range(RADIUS):
                lo_ref[which, e, 0, :, cols] = low[e * TILE : (e + 1) * TILE].astype(BF16)
                hi_ref[which, e, 0, :, cols] = high[(e + 4) * TILE : (e + 5) * TILE].astype(BF16)
            for e in range(FR_DEV):
                own = low[(e + 2) * TILE : (e + 3) * TILE] + high[e * TILE : (e + 1) * TILE]
                own_ref[e, 0, :, cols] = own.astype(BF16)

    @pl.when(t == NTILE - 1)
    def _():
        full = dot(acc_ref[...].astype(BF16), piece_order_t())
        for b in range(HL):
            r_ref[b] = full[b * BLK : (b + 1) * BLK, b * BLK : (b + 1) * BLK].astype(BF16)


def backward(q4, k4, v4, halos, rb, attn_t, probs, inv, dmix):
    out4 = jax.ShapeDtypeStruct(OUT4, BF16)
    halo = jax.ShapeDtypeStruct(HALO, BF16)
    end = (HL, BLK, BLK)
    return pl.pallas_call(
        backward_kernel,
        grid=(NTILE,),
        in_specs=[tile_spec(FR_DEV)] * 3
        + [tile_spec(RADIUS)] * 4
        + [whole((WID, WID)), col_spec(), p_spec(), inv_spec(), col_spec()],
        out_specs=[tile_spec(FR_DEV)] * 3 + [pair_spec()] * 2 + [whole(end)],
        out_shape=[out4] * 3 + [halo] * 2 + [jax.ShapeDtypeStruct(end, BF16)],
        scratch_shapes=[pltpu.VMEM((WID, WID), F32)],
        compiler_params=params(),
        cost_estimate=pl.CostEstimate(
            flops=12 * 10**9, bytes_accessed=30 * 10**6, transcendentals=0
        ),
        name="backward",
    )(q4, k4, v4, *halos, rb, attn_t, probs, inv, dmix)


def add_kernel(dk_ref, dv_ref, below_ref, above_ref, ok_ref, ov_ref):
    for which, (own, out) in enumerate(((dk_ref, ok_ref), (dv_ref, ov_ref))):
        for e in range(RADIUS):
            out[e] = (own[e].astype(F32) + below_ref[which, e].astype(F32)).astype(BF16)
            up = own[RADIUS + e].astype(F32) + above_ref[which, e].astype(F32)
            out[RADIUS + e] = up.astype(BF16)


def add_halos(dk, dv, below, above):
    return pl.pallas_call(
        add_kernel,
        grid=(NTILE,),
        in_specs=[tile_spec(FR_DEV)] * 2 + [pair_spec()] * 2,
        out_specs=[tile_spec(FR_DEV)] * 2,
        out_shape=[jax.ShapeDtypeStruct(OUT4, BF16)] * 2,
        compiler_params=params(),
        cost_estimate=pl.CostEstimate(flops=10**6, bytes_accessed=10 * 10**6, transcendentals=0),
        name="add_halos",
    )(dk, dv, below, above)


def left_kernel(perm_ref, arr_ref, g_ref, l_ref, acc_ref):
    t = pl.program_id(0)
    term = dot(arr_ref[...], g_ref[...].reshape(COLS, WID))

    @pl.when(t == 0)
    def _():
        acc_ref[...] = term

    @pl.when(t > 0)
    def _():
        acc_ref[...] += term

    @pl.when(t == NTILE - 1)
    def _():
        full = dot(placer_of(perm_ref, True), acc_ref[...].astype(BF16))
        for c in range(HL):
            l_ref[c] = full[c * BLK : (c + 1) * BLK, c * BLK : (c + 1) * BLK].astype(BF16)


def left_sum(perm, arrived, g4):
    return pl.pallas_call(
        left_kernel,
        grid=(NTILE,),
        in_specs=[smem(), col_spec(), tile_spec(FR_DEV)],
        out_specs=whole((HL, BLK, BLK)),
        out_shape=jax.ShapeDtypeStruct((HL, BLK, BLK), BF16),
        scratch_shapes=[pltpu.VMEM((WID, WID), F32)],
        compiler_params=params(),
        cost_estimate=pl.CostEstimate(flops=10**9, bytes_accessed=4 * 10**6, transcendentals=0),
        name="left_sum",
    )(perm, arrived, g4)


def project_kernel(w_ref, arr_ref, _, out_ref):
    for n in range(2):
        part = arr_ref[:, n * 2 * TILE : (n + 1) * 2 * TILE]
        out = dot(part, w_ref[...], TN).astype(BF16)
        out_ref[2 * n : 2 * n + 2] = out.reshape(2, 1, TILE, WID)


def project(w, arrived, after):
    return pl.pallas_call(
        project_kernel,
        grid=(NTILE,),
        in_specs=[whole((WID, WID)), col_spec(), pl.BlockSpec(memory_space=pl.ANY)],
        out_specs=tile_spec(FR_DEV),
        out_shape=jax.ShapeDtypeStruct(OUT4, BF16),
        compiler_params=params(),
        cost_estimate=pl.CostEstimate(flops=10**9, bytes_accessed=4 * 10**6, transcendentals=0),
        name="project",
    )(w, arrived, after)


def tm_sums(right, left, norm, projected, dk):
    count = lax.axis_size("tm")
    first = lax.axis_index("tm") % 2 == 0

    def moved(y, to):
        return lax.ppermute(y, "tm", [(i, to(i)) for i in range(count)])

    def along_x(by):
        return lambda i: (i // 8) * 8 + (i % 8 + 2 * by) % 8

    x = jnp.where(first, right, left).astype(F32)
    x = (x + moved(jnp.where(first, left, right), lambda i: i ^ 1).astype(F32)).astype(BF16)
    x = (x.astype(F32) + moved(x, lambda i: i ^ 8).astype(F32)).astype(BF16)
    x = gate(x, projected)
    one, two, three = (moved(x, along_x(by)).astype(F32) for by in (1, 2, 3))
    x = ((x.astype(F32) + two) + (one + three)).astype(BF16)
    x = gate(x, dk)
    other = moved(x, lambda i: i ^ 1).astype(F32) * norm
    x = x.astype(F32) * norm
    return jnp.where(first, x, other), jnp.where(first, other, x)


def on_device(queries, keys, values, right_blocks, left_blocks, block_perm, reach, grad_out):
    rows, width = queries.shape
    count = lax.axis_size("tm")
    n_head = lax.axis_size("head")
    up = [(i, (i + 1) % count) for i in range(count)]
    down = [((i + 1) % count, i) for i in range(count)]
    shape4 = (FR_DEV, NTILE, TILE, width)
    q4, k4, v4, g4 = (x.reshape(shape4) for x in (queries, keys, values, grad_out))
    half = (RADIUS, NTILE, TILE, width)
    cut = RADIUS * NTILE * TILE
    halos = [
        lax.ppermute(keys[rows - cut :], "tm", up).reshape(half),
        lax.ppermute(keys[:cut], "tm", down).reshape(half),
        lax.ppermute(values[rows - cut :], "tm", up).reshape(half),
        lax.ppermute(values[:cut], "tm", down).reshape(half),
    ]
    w, rb, rbt, d_arrived = prep(block_perm, left_blocks, right_blocks, g4)

    def exchange(x):
        y = lax.all_to_all(
            x.reshape(n_head, width // n_head, rows), "head", split_axis=0, concat_axis=0, tiled=True
        )
        return y.reshape(width, rows)

    dmix = exchange(d_arrived)
    attn_t, probs, inv, mixed = forward(reach, q4, k4, v4, halos, rbt)
    arrived = exchange(mixed)
    dq, dk, dv, lo, hi, right_term = backward(q4, k4, v4, halos, rb, attn_t, probs, inv, dmix)
    below = lax.ppermute(hi, "tm", up)
    above = lax.ppermute(lo, "tm", down)
    left_term = left_sum(block_perm, arrived, g4)
    projected = project(w, arrived, left_term)
    dk, dv = add_halos(dk, dv, below, above)
    norm = float(rows * count) ** (-0.5)
    d_right, d_left = tm_sums(right_term, left_term, norm, projected, dk)
    flat = (rows, width)
    return (
        projected.reshape(flat),
        dq.reshape(flat),
        dk.reshape(flat),
        dv.reshape(flat),
        d_right,
        d_left,
    )


def solution(mesh):
    in_specs = (
        P("tm", "head"),
        P("tm", "head"),
        P("tm", "head"),
        P("head", None, None),
        P("head", None, None),
        P(),
        P(),
        P("tm", "head"),
    )
    out_specs = (
        P("tm", "head"),
        P("tm", "head"),
        P("tm", "head"),
        P("tm", "head"),
        P("head", None, None),
        P("head", None, None),
    )
    return jax.shard_map(
        on_device, mesh=mesh, in_specs=in_specs, out_specs=out_specs, check_vma=False
    )
```

time: 131 us -> 123 us (0.939)
  Pallas kernels: 52.9 us -> 48.7 us
  waiting for transfers between devices: 29 us -> 25.3 us
  starting transfers between devices: 37.7 us -> 34.5 us
  other arithmetic: 2.47 us -> 4.87 us
    pallas_call x1, Pallas kernels: 18.5 us -> 10.9 us  [forward(): pl.pallas_call(forward_kernel, grid=(NTILE,), in_specs=[smem()] + [tile_s...]
    ppermute x14 -> x10, waiting for transfers between devices: 29 us -> 25.3 us  [the longest x6 15.5 us: moved(): return lax.ppermute(y, 'tm', [(i, to(i)) for i in range(count)])]
    pallas_call x1 -> x4, Pallas kernels: 6.14 us -> 9.4 us  [the longest x1 4.93 us: left_sum(): pl.pallas_call(left_kernel, grid=(NTILE,), in_specs=[smem(), col_spec(),...]
    ppermute x14 -> x10, starting transfers between devices: 18.2 us -> 14.9 us  [the longest x6 7.17 us: moved(): return lax.ppermute(y, 'tm', [(i, to(i)) for i in range(count)])]
    select_n x0 -> x2, other arithmetic: none -> 2.58 us  [the longest x1 1.67 us: tm_sums(): return (jnp.where(first, x, other), jnp.where(first, other, x))]
    mul x2 -> x0, other arithmetic: 1.41 us -> none  [tm_sum(): return x * norm]
  transfers between devices with their start and end apart: 18 -> 14, of which waited for: 5 -> 6; matrix products, arithmetic and copies ran while one was open for 2% -> 3% of each run, Pallas kernels for 37% -> 36%
where the time goes in v2:
time: 123 us; the launch traced here: 121 us
  Pallas kernels  48.7 us (40%)
  starting transfers between devices  34.5 us (28%)
  waiting for transfers between devices  25.3 us (21%)
  local copies, waits for them, and re-layouts  7.42 us (6%)
  other arithmetic  4.87 us (4%)
    pallas_call x1, Pallas kernels, backward(): pl.pallas_call(backward_kernel, grid=(NTILE,), in_specs=[tile_spec(FR_DEV...  18 us
    all_to_all x2, starting transfers between devices, exchange(): lax.all_to_all(x.reshape(n_head, width // n_head, rows), 'head', split_ax...  15.6 us
    ppermute x6, waiting for transfers between devices, moved(): return lax.ppermute(y, 'tm', [(i, to(i)) for i in range(count)])  15.5 us
    pallas_call x1, Pallas kernels, forward(): pl.pallas_call(forward_kernel, grid=(NTILE,), in_specs=[smem()] + [tile_s...  10.9 us
    ppermute x1, waiting for transfers between devices, on_device(): lax.ppermute(values[rows - cut:], 'tm', up).reshape(half)  9.76 us
    ppermute x6, starting transfers between devices, moved(): return lax.ppermute(y, 'tm', [(i, to(i)) for i in range(count)])  7.17 us
    pallas_call x1, Pallas kernels, prep(): pl.pallas_call(prep_kernel, grid=(NTILE,), in_specs=[smem(), whole((HL, B...  5.24 us
    pallas_call x1, Pallas kernels, add_halos(): pl.pallas_call(add_kernel, grid=(NTILE,), in_specs=[tile_spec(FR_DEV)] *...  5.08 us
  transfers between devices with their start and end apart: 14, of which 6 were waited for; matrix products, arithmetic and copies ran while one was open for 3% of the time, Pallas kernels for 36%

profile of v2, /device:TPU:16, one launch (start us, length us, event | category | flops | bytes accessed | tf_op | source)
XLA Modules:
  0.0 121.5 jit_solution(4754866839045686189)
XLA Ops:
  0.6 2.7 %fusion.3 = (bf16[1024,384]{1,0:T(8,128)(2,1)}, bf16[1024,384]{1,0:T(8,128)(2,1)}) fusion(bf16[2048,384]{1,0:T(8,128)(2,1)} %param.9), kind=kLoop, calls=%fused_computation.9 | loop fusion | bytes 3145728 | tf_op jit(solution)/shard_map/slice | solution.py:439
  3.3 0.0 collective-permute-start
  3.3 3.9 %collective-permute-start.1 = (bf16[1024,384]{1,0:T(8,128)(2,1)}, bf16[1024,384]{1,0:T(8,128)(2,1)}, u32[]{:S(2)}, u32[]{:S(2)}) collective-permute-start(bf16[1024,384]{1,0:T(8,128)(2,1)} %get-tuple-element.40), channel_id=1, source_target_pairs={{8,0},{16,8},{24,16},{32,24},{40,32},{48,40},{56,48},{64,56},{72,6... | collective-permute-start | bytes 2359304 | tf_op jit(solution)/shard_map/ppermute | solution.py:439
  7.2 5.2 %prep.1 = (bf16[384,384]{1,0:T(8,128)(2,1)}, bf16[384,384]{1,0:T(8,128)(2,1)}, bf16[384,384]{1,0:T(8,128)(2,1)}, bf16[384,2048]{1,0:T(8,128)(2,1)}) custom-call(s32[24]{0:T(128)} %perm_ref.3, bf16[3,128,128]{2,1,0:T(8,128)(2,1)} %left_ref.1, bf16[3,128,128]{2,1,0:T(8,128)(2,1)} %right_ref.1, bf16[4,4,128,384]{3,2,1,0:T(8,128)(2,1)} %bitcast.29), custom_call_target="tpu_custom_call" | custom-call | flops 1000000000 | bytes 4000000 | tf_op jit(solution)/shard_map/prep/pallas_call | solution.py:144
  12.4 0.0 copy-start
  12.4 8.4 %all-to-all-start.1 = ((bf16[8,48,2048]{2,1,0:T(8,128)(2,1)}), bf16[8,48,2048]{2,1,0:T(8,128)(2,1)S(1)}, u32[]{:S(2)}, u32[]{:S(2)}) async-start(bf16[8,48,2048]{2,1,0:T(8,128)(2,1)} %bitcast.25), calls=%async_computation.1 | async-start | bytes 3145728 | tf_op jit(solution)/shard_map/all_to_all | solution.py:446
  20.8 0.0 copy-done
  20.8 0.2 fusion.2
  21.0 0.1 collective-permute-start.2
  21.0 3.8 %collective-permute-start.3 = (bf16[1024,384]{1,0:T(8,128)(2,1)S(1)}, bf16[1024,384]{1,0:T(8,128)(2,1)S(1)}, u32[]{:S(2)}, u32[]{:S(2)}) collective-permute-start(bf16[1024,384]{1,0:T(8,128)(2,1)S(1)} %get-tuple-element.38), channel_id=1, source_target_pairs={{8,0},{16,8},{24,16},{32,24},{40,32},{48,40},{56,48},{64,56},{72,6... | collective-permute-start | bytes 2359304 | tf_op jit(solution)/shard_map/ppermute | solution.py:441
  24.9 0.0 collective-permute-done
  24.9 0.0 collective-permute-done.1
  24.9 9.8 %collective-permute-done.2 = bf16[1024,384]{1,0:T(8,128)(2,1)S(1)} collective-permute-done((bf16[1024,384]{1,0:T(8,128)(2,1)S(1)}, bf16[1024,384]{1,0:T(8,128)(2,1)S(1)}, u32[]{:S(2)}, u32[]{:S(2)}) %collective-permute-start.2) | collective-permute-done | bytes 786464 | tf_op jit(solution)/shard_map/ppermute | solution.py:440
  34.7 0.0 copy-start.5
  34.7 0.0 collective-permute-done.3
  34.7 0.0 copy-start.6
  34.7 0.9 copy-done.5
  35.6 0.3 copy-done.6
  35.8 10.9 %forward.1 = (bf16[384,2048]{1,0:T(8,128)(2,1)}, bf16[4,3,2,768,256]{4,3,2,1,0:T(8,128)(2,1)}, f32[4,8,512]{2,1,0:T(8,128)}, bf16[384,2048]{1,0:T(8,128)(2,1)}) custom-call(s32[24]{0:T(128)} %reach_ref.1, bf16[4,4,128,384]{3,2,1,0:T(8,128)(2,1)} %bitcast.27, bf16[4,4,128,384]{3,2,1,0:T(8,128)(2,1)} %bitcast.16, bf16[4,4,128,384]{3,2,1,0:T(8,128)(2,1)} %bitcast.18, ...), custom_call_target="tpu_custom_call" | custom-call | flops 6000000000 | bytes 20000000 | tf_op jit(solution)/shard_map/forward/pallas_call | solution.py:229
  46.8 0.0 all-to-all-done.1
  46.8 0.0 copy-start.2
  46.8 1.1 copy-done.2
  47.9 7.2 %all-to-all-start = ((bf16[8,48,2048]{2,1,0:T(8,128)(2,1)}), bf16[8,48,2048]{2,1,0:T(8,128)(2,1)S(1)}, u32[]{:S(2)}, u32[]{:S(2)}) async-start(bf16[8,48,2048]{2,1,0:T(8,128)(2,1)} %bitcast.23), calls=%async_computation | async-start | bytes 3145728 | tf_op jit(solution)/shard_map/all_to_all | solution.py:446
  55.1 18.0 %backward.1 = (bf16[4,4,128,384]{3,2,1,0:T(8,128)(2,1)}, bf16[4,4,128,384]{3,2,1,0:T(8,128)(2,1)}, bf16[4,4,128,384]{3,2,1,0:T(8,128)(2,1)}, bf16[2,2,4,128,384]...) custom-call(bf16[4,4,128,384]{3,2,1,0:T(8,128)(2,1)} %bitcast.28, ...), custom_call_target="tpu_custom_call" | custom-call | flops 12000000000 | bytes 30000000 | tf_op jit(solution)/shard_map/backward/pallas_call | solution.py:314
  73.1 0.1 collective-permute-start.4
  73.2 3.8 %collective-permute-start.5 = (bf16[2,2,4,128,384]{4,3,2,1,0:T(8,128)(2,1)}, bf16[2,2,4,128,384]{4,3,2,1,0:T(8,128)(2,1)}, u32[]{:S(2)}, u32[]{:S(2)}) collective-permute-start(bf16[2,2,4,128,384]{4,3,2,1,0:T(8,128)(2,1)} %get-tuple-element.34), channel_id=1, source_target_pairs={{8,0},{16,8},{24,16},{32,24},{40,32},{48,40},{56,48},{64,56},{72,6... | collective-permute-start | bytes 4718600 | tf_op jit(solution)/shard_map/ppermute | solution.py:456
  77.1 0.0 all-to-all-done
  77.1 0.0 copy-start.1
  77.1 1.1 copy-done.1
  78.2 0.0 copy-start.4
  78.2 4.9 %left_sum.1._ = bf16[3,128,128]{2,1,0:T(8,128)(2,1)} custom-call(s32[24]{0:T(128)} %perm_ref.3, bf16[384,2048]{1,0:T(8,128)(2,1)} %bitcast.20, bf16[4,4,128,384]{3,2,1,0:T(8,128)(2,1)} %bitcast.30), custom_call_target="tpu_custom_call" | custom-call | flops 1000000000 | bytes 4000000 | tf_op jit(solution)/shard_map/left_sum/pallas_call | solution.py:372
  83.1 0.0 copy-done.4
  83.1 0.9 broadcast_select_fusion
  84.1 0.1 collective-permute-start.6
  84.2 1.3 %collective-permute-done.6 = bf16[3,128,128]{2,1,0:T(8,128)(2,1)S(1)} collective-permute-done((bf16[3,128,128]{2,1,0:T(8,128)(2,1)S(1)}, bf16[3,128,128]{2,1,0:T(8,128)(2,1)S(1)}, u32[]{:S(2)}, u32[]{:S(2)}) %collective-permute-start.6) | collective-permute-done | bytes 98336 | tf_op jit(solution)/shard_map/ppermute | solution.py:410
  85.5 1.4 %collective-permute-start.7 = (bf16[3,128,128]{2,1,0:T(8,128)(2,1)S(1)}, bf16[3,128,128]{2,1,0:T(8,128)(2,1)S(1)}, u32[]{:S(2)}, u32[]{:S(2)}) collective-permute-start(bf16[3,128,128]{2,1,0:T(8,128)(2,1)S(1)} %add_convert_fusion.2), channel_id=1, source_target_pairs={{0,64},{8,72},{16,80},{24,88},{32,96},{40,104},{48,112},{56,120},{... | collective-permute-start | bytes 294920 | tf_op jit(solution)/shard_map/ppermute | solution.py:410
  86.9 4.5 %project.1.refs_1_ = bf16[4,4,128,384]{3,2,1,0:T(8,128)(2,1)} custom-call(bf16[384,384]{1,0:T(8,128)(2,1)} %get-tuple-element.22.w_ref, bf16[384,2048]{1,0:T(8,128)(2,1)} %bitcast.21, bf16[3,128,128]{2,1,0:T(8,128)(2,1)} %left_sum.1._), custom_call_target="tpu_custom_call" | custom-call | flops 1000000000 | bytes 4000000 | tf_op jit(solution)/shard_map/project/pallas_call | solution.py:393
  91.3 6.2 %collective-permute-done.7 = bf16[3,128,128]{2,1,0:T(8,128)(2,1)S(1)} collective-permute-done((bf16[3,128,128]{2,1,0:T(8,128)(2,1)S(1)}, bf16[3,128,128]{2,1,0:T(8,128)(2,1)S(1)}, u32[]{:S(2)}, u32[]{:S(2)}) %collective-permute-start.7) | collective-permute-done | bytes 98336 | tf_op jit(solution)/shard_map/ppermute | solution.py:410
  97.5 0.7 add_convert_fusion.1.refs_0_
  98.1 4.3 %collective-permute-start.10 = (bf16[3,128,128]{2,1,0:T(8,128)(2,1)}, bf16[3,128,128]{2,1,0:T(8,128)(2,1)S(1)}, u32[]{:S(2)}, u32[]{:S(2)}) collective-permute-start(bf16[3,128,128]{2,1,0:T(8,128)(2,1)} %gate.2), channel_id=1, source_target_pairs={{0,48},{8,56},{16,0},{24,8},{32,16},{40,24},{48,32},{56,40},{64,11... | collective-permute-start | bytes 294920 | tf_op jit(solution)/shard_map/ppermute | solution.py:410
  102.4 0.0 collective-permute-start.9
  102.4 1.5 %collective-permute-start.8 = (bf16[3,128,128]{2,1,0:T(8,128)(2,1)}, bf16[3,128,128]{2,1,0:T(8,128)(2,1)S(1)}, u32[]{:S(2)}, u32[]{:S(2)}) collective-permute-start(bf16[3,128,128]{2,1,0:T(8,128)(2,1)} %gate.2), channel_id=1, source_target_pairs={{0,32},{8,40},{16,48},{24,56},{32,0},{40,8},{48,16},{56,24},{64,96... | collective-permute-start | bytes 294920 | tf_op jit(solution)/shard_map/ppermute | solution.py:410
  103.9 1.2 collective-permute-done.10
  105.0 5.4 %collective-permute-done.9 = bf16[3,128,128]{2,1,0:T(8,128)(2,1)S(1)} collective-permute-done((bf16[3,128,128]{2,1,0:T(8,128)(2,1)}, bf16[3,128,128]{2,1,0:T(8,128)(2,1)S(1)}, u32[]{:S(2)}, u32[]{:S(2)}) %collective-permute-start.9) | collective-permute-done | bytes 98336 | tf_op jit(solution)/shard_map/ppermute | solution.py:410
  110.5 0.0 collective-permute-done.8
  110.5 1.6 %add_convert_fusion.refs_0_ = bf16[3,128,128]{2,1,0:T(8,128)(2,1)} fusion(bf16[3,128,128]{2,1,0:T(8,128)(2,1)S(1)} %collective-permute-done.10, bf16[3,128,128]{2,1,0:T(8,128)(2,1)S(1)} %collective-permute-done.9, bf16[3,128,128]{2,1,0:T(8,128)(2,1)S(1)} %collective-permute-done.8, bf16[3,128,128]{2,1,0:T(8,128)(2,1)} %gate.2), kind=kLoop, calls=%fused_computation.4 | loop fusion | flops 393216 | bytes 491520 | tf_op jit(solution)/shard_map/convert_element_type | solution.py:420
  112.0 0.0 collective-permute-done.4.below_ref
  112.0 0.0 copy-start.3
  112.0 0.0 collective-permute-done.5.above_ref
  112.1 1.1 copy-done.3
  113.2 5.1 %add_halos.1 = (bf16[4,4,128,384]{3,2,1,0:T(8,128)(2,1)}, bf16[4,4,128,384]{3,2,1,0:T(8,128)(2,1)}) custom-call(bf16[4,4,128,384]{3,2,1,0:T(8,128)(2,1)} %get-tuple-element.31.dk_ref, bf16[4,4,128,384]{3,2,1,0:T(8,128)(2,1)} %get-tuple-element.32.dv_ref, bf16[2,2,4,128,384]{4,3,2,1,0:T(8,128)(2,1)} %copy-done.3, ...), custom_call_target="tpu_custom_call" | custom-call | flops 1000000 | bytes 10000000 | tf_op jit(solution)/shard_map/add_halos/pallas_call | solution.py:340
  118.3 0.0 collective-permute-start.11
  118.3 1.5 %collective-permute-done.11 = bf16[3,128,128]{2,1,0:T(8,128)(2,1)S(1)} collective-permute-done((bf16[3,128,128]{2,1,0:T(8,128)(2,1)}, bf16[3,128,128]{2,1,0:T(8,128)(2,1)S(1)}, u32[]{:S(2)}, u32[]{:S(2)}) %collective-permute-start.11) | collective-permute-done | bytes 98336 | tf_op jit(solution)/shard_map/ppermute | solution.py:410
  119.8 1.7 %fusion = (f32[3,128,128]{2,1,0:T(8,128)}, f32[3,128,128]{2,1,0:T(8,128)}) fusion(bf16[3,128,128]{2,1,0:T(8,128)(2,1)S(1)} %collective-permute-done.11, bf16[3,128,128]{2,1,0:T(8,128)(2,1)} %gate.3, pred[]{:T(512)S(6)} %eq.5), kind=kLoop, calls=%fused_computation.1 | loop fusion | flops 294912 | bytes 589825 | tf_op jit(solution)/shard_map/jit(_where)/select_n | solution.py:424
  (3 shorter events, 0.0 us)
Async XLA Ops:
  3.3 21.6 %collective-permute-start = (bf16[1024,384]{1,0:T(8,128)(2,1)}, bf16[1024,384]{1,0:T(8,128)(2,1)}, u32[]{:S(2)}, u32[]{:S(2)}) collective-permute-start(bf16[1024,384]{1,0:T(8,128)(2,1)} %get-tuple-element.41), channel_id=1, source_target_pairs={{0,8},{8,16},{16,24},{24,32},{32,40},{40,48},{48,56},{56,64},{64,7... | collective-permute-start | bytes 2359304 | tf_op jit(solution)/shard_map/ppermute | solution.py:438
  3.3 21.6 %collective-permute-start.1 = (bf16[1024,384]{1,0:T(8,128)(2,1)}, bf16[1024,384]{1,0:T(8,128)(2,1)}, u32[]{:S(2)}, u32[]{:S(2)}) collective-permute-start(bf16[1024,384]{1,0:T(8,128)(2,1)} %get-tuple-element.40), channel_id=1, source_target_pairs={{8,0},{16,8},{24,16},{32,24},{40,32},{48,40},{56,48},{64,56},{72,6... | collective-permute-start | bytes 2359304 | tf_op jit(solution)/shard_map/ppermute | solution.py:439
  12.4 8.4 %copy-start = (bf16[2048,384]{1,0:T(8,128)(2,1)S(1)}, bf16[2048,384]{1,0:T(8,128)(2,1)}, u32[]{:S(2)}) copy-start(bf16[2048,384]{1,0:T(8,128)(2,1)} %param.10) | copy-start | bytes 4718596
  12.4 34.4 %all-to-all-start.1 = ((bf16[8,48,2048]{2,1,0:T(8,128)(2,1)}), bf16[8,48,2048]{2,1,0:T(8,128)(2,1)S(1)}, u32[]{:S(2)}, u32[]{:S(2)}) async-start(bf16[8,48,2048]{2,1,0:T(8,128)(2,1)} %bitcast.25), calls=%async_computation.1 | async-start | bytes 3145728 | tf_op jit(solution)/shard_map/all_to_all | solution.py:446
  21.0 13.7 %collective-permute-start.2 = (bf16[1024,384]{1,0:T(8,128)(2,1)S(1)}, bf16[1024,384]{1,0:T(8,128)(2,1)S(1)}, u32[]{:S(2)}, u32[]{:S(2)}) collective-permute-start(bf16[1024,384]{1,0:T(8,128)(2,1)S(1)} %get-tuple-element.39), channel_id=1, source_target_pairs={{0,8},{8,16},{16,24},{24,32},{32,40},{40,48},{48,56},{56,64},{64,7... | collective-permute-start | bytes 2359304 | tf_op jit(solution)/shard_map/ppermute | solution.py:440
  21.0 13.6 %collective-permute-start.3 = (bf16[1024,384]{1,0:T(8,128)(2,1)S(1)}, bf16[1024,384]{1,0:T(8,128)(2,1)S(1)}, u32[]{:S(2)}, u32[]{:S(2)}) collective-permute-start(bf16[1024,384]{1,0:T(8,128)(2,1)S(1)} %get-tuple-element.38), channel_id=1, source_target_pairs={{8,0},{16,8},{24,16},{32,24},{40,32},{48,40},{56,48},{64,56},{72,6... | collective-permute-start | bytes 2359304 | tf_op jit(solution)/shard_map/ppermute | solution.py:441
  34.7 0.9 copy-start.5
  34.7 1.2 copy-start.6
  46.8 1.1 copy-start.2
  47.9 29.2 %all-to-all-start = ((bf16[8,48,2048]{2,1,0:T(8,128)(2,1)}), bf16[8,48,2048]{2,1,0:T(8,128)(2,1)S(1)}, u32[]{:S(2)}, u32[]{:S(2)}) async-start(bf16[8,48,2048]{2,1,0:T(8,128)(2,1)} %bitcast.23), calls=%async_computation | async-start | bytes 3145728 | tf_op jit(solution)/shard_map/all_to_all | solution.py:446
  73.1 38.9 %collective-permute-start.4 = (bf16[2,2,4,128,384]{4,3,2,1,0:T(8,128)(2,1)}, bf16[2,2,4,128,384]{4,3,2,1,0:T(8,128)(2,1)S(1)}, u32[]{:S(2)}, u32[]{:S(2)}) collective-permute-start(bf16[2,2,4,128,384]{4,3,2,1,0:T(8,128)(2,1)} %get-tuple-element.33), channel_id=1, source_target_pairs={{0,8},{8,16},{16,24},{24,32},{32,40},{40,48},{48,56},{56,64},{64,7... | collective-permute-start | bytes 4718600 | tf_op jit(solution)/shard_map/ppermute | solution.py:455
  73.2 38.8 %collective-permute-start.5 = (bf16[2,2,4,128,384]{4,3,2,1,0:T(8,128)(2,1)}, bf16[2,2,4,128,384]{4,3,2,1,0:T(8,128)(2,1)}, u32[]{:S(2)}, u32[]{:S(2)}) collective-permute-start(bf16[2,2,4,128,384]{4,3,2,1,0:T(8,128)(2,1)} %get-tuple-element.34), channel_id=1, source_target_pairs={{8,0},{16,8},{24,16},{32,24},{40,32},{48,40},{56,48},{64,56},{72,6... | collective-permute-start | bytes 4718600 | tf_op jit(solution)/shard_map/ppermute | solution.py:456
  77.1 1.1 copy-start.1
  78.2 4.9 %copy-start.4 = (bf16[3,128,128]{2,1,0:T(8,128)(2,1)S(1)}, bf16[3,128,128]{2,1,0:T(8,128)(2,1)}, u32[]{:S(2)}) copy-start(bf16[3,128,128]{2,1,0:T(8,128)(2,1)} %get-tuple-element.37) | copy-start | bytes 294916
  84.1 1.4 %collective-permute-start.6 = (bf16[3,128,128]{2,1,0:T(8,128)(2,1)S(1)}, bf16[3,128,128]{2,1,0:T(8,128)(2,1)S(1)}, u32[]{:S(2)}, u32[]{:S(2)}) collective-permute-start(bf16[3,128,128]{2,1,0:T(8,128)(2,1)S(1)} %broadcast_select_fusion), channel_id=1, source_target_pairs={{0,8},{8,0},{16,24},{24,16},{32,40},{40,32},{48,56},{56,48},{64,72... | collective-permute-start | bytes 294920 | tf_op jit(solution)/shard_map/ppermute | solution.py:410
  85.5 12.0 %collective-permute-start.7 = (bf16[3,128,128]{2,1,0:T(8,128)(2,1)S(1)}, bf16[3,128,128]{2,1,0:T(8,128)(2,1)S(1)}, u32[]{:S(2)}, u32[]{:S(2)}) collective-permute-start(bf16[3,128,128]{2,1,0:T(8,128)(2,1)S(1)} %add_convert_fusion.2), channel_id=1, source_target_pairs={{0,64},{8,72},{16,80},{24,88},{32,96},{40,104},{48,112},{56,120},{... | collective-permute-start | bytes 294920 | tf_op jit(solution)/shard_map/ppermute | solution.py:410
  98.1 6.9 %collective-permute-start.10 = (bf16[3,128,128]{2,1,0:T(8,128)(2,1)}, bf16[3,128,128]{2,1,0:T(8,128)(2,1)S(1)}, u32[]{:S(2)}, u32[]{:S(2)}) collective-permute-start(bf16[3,128,128]{2,1,0:T(8,128)(2,1)} %gate.2), channel_id=1, source_target_pairs={{0,48},{8,56},{16,0},{24,8},{32,16},{40,24},{48,32},{56,40},{64,11... | collective-permute-start | bytes 294920 | tf_op jit(solution)/shard_map/ppermute | solution.py:410
  102.4 8.1 %collective-permute-start.9 = (bf16[3,128,128]{2,1,0:T(8,128)(2,1)}, bf16[3,128,128]{2,1,0:T(8,128)(2,1)S(1)}, u32[]{:S(2)}, u32[]{:S(2)}) collective-permute-start(bf16[3,128,128]{2,1,0:T(8,128)(2,1)} %gate.2), channel_id=1, source_target_pairs={{0,16},{8,24},{16,32},{24,40},{32,48},{40,56},{48,0},{56,8},{64,80... | collective-permute-start | bytes 294920 | tf_op jit(solution)/shard_map/ppermute | solution.py:410
  102.4 8.1 %collective-permute-start.8 = (bf16[3,128,128]{2,1,0:T(8,128)(2,1)}, bf16[3,128,128]{2,1,0:T(8,128)(2,1)S(1)}, u32[]{:S(2)}, u32[]{:S(2)}) collective-permute-start(bf16[3,128,128]{2,1,0:T(8,128)(2,1)} %gate.2), channel_id=1, source_target_pairs={{0,32},{8,40},{16,48},{24,56},{32,0},{40,8},{48,16},{56,24},{64,96... | collective-permute-start | bytes 294920 | tf_op jit(solution)/shard_map/ppermute | solution.py:410
  112.0 1.1 copy-start.3
  118.3 1.5 %collective-permute-start.11 = (bf16[3,128,128]{2,1,0:T(8,128)(2,1)}, bf16[3,128,128]{2,1,0:T(8,128)(2,1)S(1)}, u32[]{:S(2)}, u32[]{:S(2)}) collective-permute-start(bf16[3,128,128]{2,1,0:T(8,128)(2,1)} %gate.3), channel_id=1, source_target_pairs={{0,8},{8,0},{16,24},{24,16},{32,40},{40,32},{48,56},{56,48},{64,72... | collective-permute-start | bytes 294920 | tf_op jit(solution)/shard_map/ppermute | solution.py:410

commit v3 on v2

--- a/solution.py
+++ b/solution.py
@@ -35,9 +35,9 @@
     return lax.dot_general(a, b, dims, preferred_element_type=F32)
 
 
-def params():
+def params(mib=56):
     return pltpu.CompilerParams(
-        vmem_limit_bytes=VMEM, dimension_semantics=("arbitrary",)
+        vmem_limit_bytes=mib * 1024 * 1024, dimension_semantics=("arbitrary",)
     )
 
 
@@ -127,30 +127,48 @@
 OUT4 = (FR_DEV, NTILE, TILE, WID)
 
 
-def prep_kernel(perm_ref, left_ref, right_ref, g_ref, w_ref, rb_ref, rbt_ref, da_ref):
+def prep_kernel(perm_ref, left_ref, g_ref, w_ref, da_ref):
     @pl.when(pl.program_id(0) == 0)
     def _():
         w_ref[...] = dot(placer_of(perm_ref, False), block_diag(left_ref[...])).astype(BF16)
-        rb = dot(block_diag(right_ref[...]), piece_order()).astype(BF16)
-        rb_ref[...] = rb
-        rbt_ref[...] = turned(rb)
-
-    g = g_ref[...].reshape(COLS, WID)
-    da_ref[...] = dot(w_ref[...], g, NT).astype(BF16)
-
-
-def prep(perm, left, right, g4):
-    square = jax.ShapeDtypeStruct((WID, WID), BF16)
+
+    da_ref[...] = dot(w_ref[...], g_ref[...].reshape(COLS, WID), NT).astype(BF16)
+
+
+def prep(perm, left, g4):
     return pl.pallas_call(
         prep_kernel,
         grid=(NTILE,),
-        in_specs=[smem(), whole((HL, BLK, BLK)), whole((HL, BLK, BLK)), tile_spec(FR_DEV)],
-        out_specs=[whole((WID, WID))] * 3 + [col_spec()],
-        out_shape=[square] * 3 + [jax.ShapeDtypeStruct((WID, ROWS), BF16)],
+        in_specs=[smem(), whole((HL, BLK, BLK)), tile_spec(FR_DEV)],
+        out_specs=[whole((WID, WID)), col_spec()],
+        out_shape=[
+            jax.ShapeDtypeStruct((WID, WID), BF16),
+            jax.ShapeDtypeStruct((WID, ROWS), BF16),
+        ],
         compiler_params=params(),
         cost_estimate=pl.CostEstimate(flops=10**9, bytes_accessed=4 * 10**6, transcendentals=0),
         name="prep",
-    )(perm, left, right, g4)
+    )(perm, left, g4)
+
+
+def orders_kernel(perm_ref, right_ref, rb_ref, rbt_ref, back_ref):
+    rb = dot(block_diag(right_ref[...]), piece_order()).astype(BF16)
+    rb_ref[...] = rb
+    rbt_ref[...] = turned(rb)
+    back_ref[...] = placer_of(perm_ref, True)
+
+
+def orders(perm, right):
+    square = jax.ShapeDtypeStruct((WID, WID), BF16)
+    return pl.pallas_call(
+        orders_kernel,
+        in_specs=[smem(), pl.BlockSpec(memory_space=pltpu.VMEM)],
+        out_specs=[pl.BlockSpec(memory_space=pltpu.VMEM)] * 3,
+        out_shape=[square] * 3,
+        compiler_params=pltpu.CompilerParams(vmem_limit_bytes=VMEM),
+        cost_estimate=pl.CostEstimate(flops=3 * 10**8, bytes_accessed=10**6, transcendentals=0),
+        name="orders",
+    )(perm, right)
 
 
 def ext_rows(lo, own, hi, which, h):
@@ -343,13 +361,13 @@
         in_specs=[tile_spec(FR_DEV)] * 2 + [pair_spec()] * 2,
         out_specs=[tile_spec(FR_DEV)] * 2,
         out_shape=[jax.ShapeDtypeStruct(OUT4, BF16)] * 2,
-        compiler_params=params(),
+        compiler_params=params(16),
         cost_estimate=pl.CostEstimate(flops=10**6, bytes_accessed=10 * 10**6, transcendentals=0),
         name="add_halos",
     )(dk, dv, below, above)
 
 
-def left_kernel(perm_ref, arr_ref, g_ref, l_ref, acc_ref):
+def left_kernel(back_ref, arr_ref, g_ref, l_ref, acc_ref):
     t = pl.program_id(0)
     term = dot(arr_ref[...], g_ref[...].reshape(COLS, WID))
 
@@ -363,23 +381,23 @@
 
     @pl.when(t == NTILE - 1)
     def _():
-        full = dot(placer_of(perm_ref, True), acc_ref[...].astype(BF16))
+        full = dot(back_ref[...], acc_ref[...].astype(BF16))
         for c in range(HL):
             l_ref[c] = full[c * BLK : (c + 1) * BLK, c * BLK : (c + 1) * BLK].astype(BF16)
 
 
-def left_sum(perm, arrived, g4):
+def left_sum(back, arrived, g4):
     return pl.pallas_call(
         left_kernel,
         grid=(NTILE,),
-        in_specs=[smem(), col_spec(), tile_spec(FR_DEV)],
+        in_specs=[whole((WID, WID)), col_spec(), tile_spec(FR_DEV)],
         out_specs=whole((HL, BLK, BLK)),
         out_shape=jax.ShapeDtypeStruct((HL, BLK, BLK), BF16),
         scratch_shapes=[pltpu.VMEM((WID, WID), F32)],
-        compiler_params=params(),
+        compiler_params=params(16),
         cost_estimate=pl.CostEstimate(flops=10**9, bytes_accessed=4 * 10**6, transcendentals=0),
         name="left_sum",
-    )(perm, arrived, g4)
+    )(back, arrived, g4)
 
 
 def project_kernel(w_ref, arr_ref, _, out_ref):
@@ -396,7 +414,7 @@
         in_specs=[whole((WID, WID)), col_spec(), pl.BlockSpec(memory_space=pl.ANY)],
         out_specs=tile_spec(FR_DEV),
         out_shape=jax.ShapeDtypeStruct(OUT4, BF16),
-        compiler_params=params(),
+        compiler_params=params(16),
         cost_estimate=pl.CostEstimate(flops=10**9, bytes_accessed=4 * 10**6, transcendentals=0),
         name="project",
     )(w, arrived, after)
@@ -414,11 +432,11 @@
 
     x = jnp.where(first, right, left).astype(F32)
     x = (x + moved(jnp.where(first, left, right), lambda i: i ^ 1).astype(F32)).astype(BF16)
-    x = (x.astype(F32) + moved(x, lambda i: i ^ 8).astype(F32)).astype(BF16)
-    x = gate(x, projected)
     one, two, three = (moved(x, along_x(by)).astype(F32) for by in (1, 2, 3))
     x = ((x.astype(F32) + two) + (one + three)).astype(BF16)
-    x = gate(x, dk)
+    x = gate(x, projected)
+    far = gate(moved(x, lambda i: i ^ 8), dk)
+    x = (x.astype(F32) + far.astype(F32)).astype(BF16)
     other = moved(x, lambda i: i ^ 1).astype(F32) * norm
     x = x.astype(F32) * norm
     return jnp.where(first, x, other), jnp.where(first, other, x)
@@ -440,7 +458,7 @@
         lax.ppermute(values[rows - cut :], "tm", up).reshape(half),
         lax.ppermute(values[:cut], "tm", down).reshape(half),
     ]
-    w, rb, rbt, d_arrived = prep(block_perm, left_blocks, right_blocks, g4)
+    w, d_arrived = prep(block_perm, left_blocks, g4)
 
     def exchange(x):
         y = lax.all_to_all(
@@ -449,12 +467,13 @@
         return y.reshape(width, rows)
 
     dmix = exchange(d_arrived)
+    rb, rbt, back = orders(block_perm, right_blocks)
     attn_t, probs, inv, mixed = forward(reach, q4, k4, v4, halos, rbt)
     arrived = exchange(mixed)
     dq, dk, dv, lo, hi, right_term = backward(q4, k4, v4, halos, rb, attn_t, probs, inv, dmix)
     below = lax.ppermute(hi, "tm", up)
     above = lax.ppermute(lo, "tm", down)
-    left_term = left_sum(block_perm, arrived, g4)
+    left_term = left_sum(back, arrived, g4)
     projected = project(w, arrived, left_term)
     dk, dv = add_halos(dk, dv, below, above)
     norm = float(rows * count) ** (-0.5)

time: 123 us -> 111 us (0.902)
  waiting for transfers between devices: 25.3 us -> 20.6 us
  Pallas kernels: 48.7 us -> 46 us
  starting transfers between devices: 34.5 us -> 32 us
  other arithmetic: 4.87 us -> 2.46 us
    ppermute x1, waiting for transfers between devices: 9.76 us -> 7.08 us  [on_device(): lax.ppermute(values[rows - cut:], 'tm', up).reshape(half)]
    ppermute x6, starting transfers between devices: 7.17 us -> 4.74 us  [moved(): return lax.ppermute(y, 'tm', [(i, to(i)) for i in range(count)])]
    ppermute x6, waiting for transfers between devices: 15.5 us -> 13.5 us  [moved(): return lax.ppermute(y, 'tm', [(i, to(i)) for i in range(count)])]
    pallas_call x1, Pallas kernels: 4.47 us -> 2.92 us  [project(): pl.pallas_call(project_kernel, grid=(NTILE,), in_specs=[whole((WID, WID))...]
    pallas_call x1 -> x2, Pallas kernels: 4.93 us -> 5.04 us  [the longest x1 2.69 us: orders(): pl.pallas_call(orders_kernel, in_specs=[smem(), pl.BlockSpec(memory_space...]
    unnamed x14 -> x24, local copies, waits for them, and re-layouts: 4.6 us -> 4.66 us
  transfers between devices with their start and end apart: 14 -> 14, of which waited for: 6 -> 4; matrix products, arithmetic and copies ran while one was open for 3% -> 1% of each run, Pallas kernels for 36% -> 42%
where the time goes in v3:
time: 111 us; the launch traced here: 109 us
  Pallas kernels  46 us (41%)
  starting transfers between devices  32 us (29%)
  waiting for transfers between devices  20.6 us (19%)
  local copies, waits for them, and re-layouts  7.48 us (7%)
  other arithmetic  2.46 us (2%)
    pallas_call x1, Pallas kernels, backward(): pl.pallas_call(backward_kernel, grid=(NTILE,), in_specs=[tile_spec(FR_DEV...  18.1 us
    all_to_all x2, starting transfers between devices, exchange(): lax.all_to_all(x.reshape(n_head, width // n_head, rows), 'head', split_ax...  15.6 us
    ppermute x6, waiting for transfers between devices, moved(): return lax.ppermute(y, 'tm', [(i, to(i)) for i in range(count)])  13.5 us
    pallas_call x1, Pallas kernels, forward(): pl.pallas_call(forward_kernel, grid=(NTILE,), in_specs=[smem()] + [tile_s...  10.9 us
    ppermute x1, waiting for transfers between devices, on_device(): lax.ppermute(values[rows - cut:], 'tm', up).reshape(half)  7.08 us
    ppermute x6, starting transfers between devices, moved(): return lax.ppermute(y, 'tm', [(i, to(i)) for i in range(count)])  4.74 us
    pallas_call x1, Pallas kernels, prep(): pl.pallas_call(prep_kernel, grid=(NTILE,), in_specs=[smem(), whole((HL, B...  4.7 us
    unnamed x24, local copies, waits for them, and re-layouts  4.66 us
  transfers between devices with their start and end apart: 14, of which 4 were waited for; matrix products, arithmetic and copies ran while one was open for 1% of the time, Pallas kernels for 42%

profile of v3, /device:TPU:16, one launch (start us, length us, event | category | flops | bytes accessed | tf_op | source)
XLA Modules:
  0.0 109.4 jit_solution(16954256720736991744)
XLA Ops:
  0.6 2.7 %fusion.3 = (bf16[1024,384]{1,0:T(8,128)(2,1)}, bf16[1024,384]{1,0:T(8,128)(2,1)}) fusion(bf16[2048,384]{1,0:T(8,128)(2,1)} %param.9), kind=kLoop, calls=%fused_computation.9 | loop fusion | bytes 3145728 | tf_op jit(solution)/shard_map/slice | solution.py:457
  3.3 0.0 collective-permute-start
  3.3 3.9 %collective-permute-start.1 = (bf16[1024,384]{1,0:T(8,128)(2,1)}, bf16[1024,384]{1,0:T(8,128)(2,1)}, u32[]{:S(2)}, u32[]{:S(2)}) collective-permute-start(bf16[1024,384]{1,0:T(8,128)(2,1)} %get-tuple-element.42), channel_id=1, source_target_pairs={{8,0},{16,8},{24,16},{32,24},{40,32},{48,40},{56,48},{64,56},{72,6... | collective-permute-start | bytes 2359304 | tf_op jit(solution)/shard_map/ppermute | solution.py:457
  7.2 4.7 %prep.1 = (bf16[384,384]{1,0:T(8,128)(2,1)}, bf16[384,2048]{1,0:T(8,128)(2,1)}) custom-call(s32[24]{0:T(128)} %perm_ref.3, bf16[3,128,128]{2,1,0:T(8,128)(2,1)} %left_ref.1, bf16[4,4,128,384]{3,2,1,0:T(8,128)(2,1)} %bitcast.18), custom_call_target="tpu_custom_call" | custom-call | flops 1000000000 | bytes 4000000 | tf_op jit(solution)/shard_map/prep/pallas_call | solution.py:139
  11.9 0.0 copy-start.5
  11.9 8.4 %all-to-all-start.1 = ((bf16[8,48,2048]{2,1,0:T(8,128)(2,1)}), bf16[8,48,2048]{2,1,0:T(8,128)(2,1)S(1)}, u32[]{:S(2)}, u32[]{:S(2)}) async-start(bf16[8,48,2048]{2,1,0:T(8,128)(2,1)} %bitcast.27), calls=%async_computation.1 | async-start | bytes 3145728 | tf_op jit(solution)/shard_map/all_to_all | solution.py:464
  20.3 0.0 copy-done.5
  20.3 0.2 fusion.2
  20.4 0.1 collective-permute-start.2
  20.5 3.8 %collective-permute-start.3 = (bf16[1024,384]{1,0:T(8,128)(2,1)S(1)}, bf16[1024,384]{1,0:T(8,128)(2,1)S(1)}, u32[]{:S(2)}, u32[]{:S(2)}) collective-permute-start(bf16[1024,384]{1,0:T(8,128)(2,1)S(1)} %get-tuple-element.40), channel_id=1, source_target_pairs={{8,0},{16,8},{24,16},{32,24},{40,32},{48,40},{56,48},{64,56},{72,6... | collective-permute-start | bytes 2359304 | tf_op jit(solution)/shard_map/ppermute | solution.py:459
  24.4 2.7 %orders.1 = (bf16[384,384]{1,0:T(8,128)(2,1)}, bf16[384,384]{1,0:T(8,128)(2,1)}, bf16[384,384]{1,0:T(8,128)(2,1)}) custom-call(s32[24]{0:T(128)} %perm_ref.3, bf16[3,128,128]{2,1,0:T(8,128)(2,1)} %right_ref.1), custom_call_target="tpu_custom_call" | custom-call | flops 300000000 | bytes 1000000 | tf_op jit(solution)/shard_map/orders/pallas_call | solution.py:163
  27.0 0.0 collective-permute-done
  27.0 0.0 collective-permute-done.1
  27.1 7.1 %collective-permute-done.2 = bf16[1024,384]{1,0:T(8,128)(2,1)S(1)} collective-permute-done((bf16[1024,384]{1,0:T(8,128)(2,1)S(1)}, bf16[1024,384]{1,0:T(8,128)(2,1)S(1)}, u32[]{:S(2)}, u32[]{:S(2)}) %collective-permute-start.2) | collective-permute-done | bytes 786464 | tf_op jit(solution)/shard_map/ppermute | solution.py:458
  34.1 0.0 copy-start.10
  34.1 0.0 collective-permute-done.3
  34.1 0.0 copy-start.11
  34.1 0.9 copy-done.10
  35.0 0.3 copy-done.11
  35.3 10.9 %forward.1 = (bf16[384,2048]{1,0:T(8,128)(2,1)}, bf16[4,3,2,768,256]{4,3,2,1,0:T(8,128)(2,1)}, f32[4,8,512]{2,1,0:T(8,128)}, bf16[384,2048]{1,0:T(8,128)(2,1)}) custom-call(s32[24]{0:T(128)} %reach_ref.1, bf16[4,4,128,384]{3,2,1,0:T(8,128)(2,1)} %bitcast.29, bf16[4,4,128,384]{3,2,1,0:T(8,128)(2,1)} %bitcast.20, bf16[4,4,128,384]{3,2,1,0:T(8,128)(2,1)} %bitcast.22, ...), custom_call_target="tpu_custom_call" | custom-call | flops 6000000000 | bytes 20000000 | tf_op jit(solution)/shard_map/forward/pallas_call | solution.py:247
  46.2 0.0 all-to-all-done.1
  46.2 0.0 copy-start.6
  46.2 1.1 %copy-done.6 = bf16[8,48,2048]{2,1,0:T(8,128)(2,1)} copy-done((bf16[8,48,2048]{2,1,0:T(8,128)(2,1)}, bf16[8,48,2048]{2,1,0:T(8,128)(2,1)S(1)}, u32[]{:S(2)}) %copy-start.6) | copy-done | bytes 1572888
  47.4 7.2 %all-to-all-start = ((bf16[8,48,2048]{2,1,0:T(8,128)(2,1)}), bf16[8,48,2048]{2,1,0:T(8,128)(2,1)S(1)}, u32[]{:S(2)}, u32[]{:S(2)}) async-start(bf16[8,48,2048]{2,1,0:T(8,128)(2,1)} %bitcast.24), calls=%async_computation | async-start | bytes 3145728 | tf_op jit(solution)/shard_map/all_to_all | solution.py:464
  54.6 0.0 copy-start.4
  54.6 18.1 %backward.1 = (bf16[4,4,128,384]{3,2,1,0:T(8,128)(2,1)}, bf16[4,4,128,384]{3,2,1,0:T(8,128)(2,1)}, bf16[4,4,128,384]{3,2,1,0:T(8,128)(2,1)}, bf16[2,2,4,128,384]...) custom-call(bf16[4,4,128,384]{3,2,1,0:T(8,128)(2,1)} %bitcast.30, ...), custom_call_target="tpu_custom_call" | custom-call | flops 12000000000 | bytes 30000000 | tf_op jit(solution)/shard_map/backward/pallas_call | solution.py:332
  72.6 0.1 collective-permute-start.4
  72.7 3.8 %collective-permute-start.5 = (bf16[2,2,4,128,384]{4,3,2,1,0:T(8,128)(2,1)}, bf16[2,2,4,128,384]{4,3,2,1,0:T(8,128)(2,1)}, u32[]{:S(2)}, u32[]{:S(2)}) collective-permute-start(bf16[2,2,4,128,384]{4,3,2,1,0:T(8,128)(2,1)} %get-tuple-element.36), channel_id=1, source_target_pairs={{8,0},{16,8},{24,16},{32,24},{40,32},{48,40},{56,48},{64,56},{72,6... | collective-permute-start | bytes 4718600 | tf_op jit(solution)/shard_map/ppermute | solution.py:475
  76.6 0.0 all-to-all-done
  76.6 0.0 copy-done.4
  76.6 0.0 copy-start.2
  76.6 1.4 %copy-done.2 = bf16[2048,384]{1,0:T(8,128)(2,1)S(1)} copy-done((bf16[2048,384]{1,0:T(8,128)(2,1)S(1)}, bf16[2048,384]{1,0:T(8,128)(2,1)}, u32[]{:S(2)}) %copy-start.2) | copy-done | bytes 1572888
  78.0 0.0 copy-start.9
  78.0 0.0 copy-start.3
  78.0 2.4 %left_sum.1._ = bf16[3,128,128]{2,1,0:T(8,128)(2,1)S(1)} custom-call(bf16[384,384]{1,0:T(8,128)(2,1)S(1)} %copy-done.4, bf16[384,2048]{1,0:T(8,128)(2,1)S(1)} %bitcast.16, bf16[4,4,128,384]{3,2,1,0:T(8,128)(2,1)S(1)} %bitcast.19), custom_call_target="tpu_custom_call" | custom-call | flops 1000000000 | bytes 4000000 | tf_op jit(solution)/shard_map/left_sum/pallas_call | solution.py:390
  80.3 0.0 copy-done.9
  80.4 0.1 collective-permute-start.6
  80.5 1.3 %collective-permute-done.6 = bf16[3,128,128]{2,1,0:T(8,128)(2,1)S(1)} collective-permute-done((bf16[3,128,128]{2,1,0:T(8,128)(2,1)S(1)}, bf16[3,128,128]{2,1,0:T(8,128)(2,1)S(1)}, u32[]{:S(2)}, u32[]{:S(2)}) %collective-permute-start.6) | collective-permute-done | bytes 98336 | tf_op jit(solution)/shard_map/ppermute | solution.py:428
  81.8 1.8 %collective-permute-start.9 = (bf16[3,128,128]{2,1,0:T(8,128)(2,1)S(1)}, bf16[3,128,128]{2,1,0:T(8,128)(2,1)S(1)}, u32[]{:S(2)}, u32[]{:S(2)}) collective-permute-start(bf16[3,128,128]{2,1,0:T(8,128)(2,1)S(1)} %add_convert_fusion.2), channel_id=1, source_target_pairs={{0,48},{8,56},{16,0},{24,8},{32,16},{40,24},{48,32},{56,40},{64,11... | collective-permute-start | bytes 294920 | tf_op jit(solution)/shard_map/ppermute | solution.py:428
  83.6 0.3 collective-permute-start.8
  83.9 1.2 %collective-permute-start.7 = (bf16[3,128,128]{2,1,0:T(8,128)(2,1)S(1)}, bf16[3,128,128]{2,1,0:T(8,128)(2,1)S(1)}, u32[]{:S(2)}, u32[]{:S(2)}) collective-permute-start(bf16[3,128,128]{2,1,0:T(8,128)(2,1)S(1)} %add_convert_fusion.2), channel_id=1, source_target_pairs={{0,32},{8,40},{16,48},{24,56},{32,0},{40,8},{48,16},{56,24},{64,96... | collective-permute-start | bytes 294920 | tf_op jit(solution)/shard_map/ppermute | solution.py:428
  85.1 0.0 copy-done.3
  85.1 0.0 copy-start.1
  85.1 2.9 %project.1.refs_1_ = bf16[4,4,128,384]{3,2,1,0:T(8,128)(2,1)} custom-call(bf16[384,384]{1,0:T(8,128)(2,1)S(1)} %copy-done.3, bf16[384,2048]{1,0:T(8,128)(2,1)S(1)} %bitcast.17, bf16[3,128,128]{2,1,0:T(8,128)(2,1)S(1)} %left_sum.1._), custom_call_target="tpu_custom_call" | custom-call | flops 1000000000 | bytes 4000000 | tf_op jit(solution)/shard_map/project/pallas_call | solution.py:411
  88.0 0.0 copy-start
  88.0 10.9 %collective-permute-done.9 = bf16[3,128,128]{2,1,0:T(8,128)(2,1)S(1)} collective-permute-done((bf16[3,128,128]{2,1,0:T(8,128)(2,1)S(1)}, bf16[3,128,128]{2,1,0:T(8,128)(2,1)S(1)}, u32[]{:S(2)}, u32[]{:S(2)}) %collective-permute-start.9) | collective-permute-done | bytes 98336 | tf_op jit(solution)/shard_map/ppermute | solution.py:428
  98.9 0.0 collective-permute-done.8
  98.9 0.0 collective-permute-done.7
  98.9 0.7 add_convert_fusion.1.refs_0_
  99.6 1.3 %collective-permute-start.10 = (bf16[3,128,128]{2,1,0:T(8,128)(2,1)}, bf16[3,128,128]{2,1,0:T(8,128)(2,1)S(1)}, u32[]{:S(2)}, u32[]{:S(2)}) collective-permute-start(bf16[3,128,128]{2,1,0:T(8,128)(2,1)} %gate.2), channel_id=1, source_target_pairs={{0,64},{8,72},{16,80},{24,88},{32,96},{40,104},{48,112},{56,120},{... | collective-permute-start | bytes 294920 | tf_op jit(solution)/shard_map/ppermute | solution.py:428
  100.9 0.0 collective-permute-done.4.below_ref
  100.9 0.0 collective-permute-done.5.above_ref
  100.9 0.0 copy-done.1
  100.9 0.0 copy-done
  100.9 4.4 %add_halos.1 = (bf16[4,4,128,384]{3,2,1,0:T(8,128)(2,1)}, bf16[4,4,128,384]{3,2,1,0:T(8,128)(2,1)}) custom-call(bf16[4,4,128,384]{3,2,1,0:T(8,128)(2,1)S(1)} %copy-done, bf16[4,4,128,384]{3,2,1,0:T(8,128)(2,1)S(1)} %copy-done.1, bf16[2,2,4,128,384]{4,3,2,1,0:T(8,128)(2,1)S(1)} %collective-permute-done.4.below_ref, ...), custom_call_target="tpu_custom_call" | custom-call | flops 1000000 | bytes 10000000 | tf_op jit(solution)/shard_map/add_halos/pallas_call | solution.py:358
  105.3 0.0 copy-start.7
  105.3 0.0 collective-permute-done.10.refs_0_
  105.3 0.0 copy-start.8
  105.4 0.6 copy-done.8
  106.0 0.3 copy-done.7
  106.3 0.9 add_convert_fusion
  107.2 0.1 collective-permute-start.11
  107.3 1.3 %collective-permute-done.11 = bf16[3,128,128]{2,1,0:T(8,128)(2,1)S(1)} collective-permute-done((bf16[3,128,128]{2,1,0:T(8,128)(2,1)S(1)}, bf16[3,128,128]{2,1,0:T(8,128)(2,1)S(1)}, u32[]{:S(2)}, u32[]{:S(2)}) %collective-permute-start.11) | collective-permute-done | bytes 98336 | tf_op jit(solution)/shard_map/ppermute | solution.py:428
  108.6 0.8 fusion
  (4 shorter events, 0.1 us)
Async XLA Ops:
  3.3 23.8 %collective-permute-start = (bf16[1024,384]{1,0:T(8,128)(2,1)}, bf16[1024,384]{1,0:T(8,128)(2,1)}, u32[]{:S(2)}, u32[]{:S(2)}) collective-permute-start(bf16[1024,384]{1,0:T(8,128)(2,1)} %get-tuple-element.43), channel_id=1, source_target_pairs={{0,8},{8,16},{16,24},{24,32},{32,40},{40,48},{48,56},{56,64},{64,7... | collective-permute-start | bytes 2359304 | tf_op jit(solution)/shard_map/ppermute | solution.py:456
  3.3 23.8 %collective-permute-start.1 = (bf16[1024,384]{1,0:T(8,128)(2,1)}, bf16[1024,384]{1,0:T(8,128)(2,1)}, u32[]{:S(2)}, u32[]{:S(2)}) collective-permute-start(bf16[1024,384]{1,0:T(8,128)(2,1)} %get-tuple-element.42), channel_id=1, source_target_pairs={{8,0},{16,8},{24,16},{32,24},{40,32},{48,40},{56,48},{64,56},{72,6... | collective-permute-start | bytes 2359304 | tf_op jit(solution)/shard_map/ppermute | solution.py:457
  11.9 8.4 %copy-start.5 = (bf16[2048,384]{1,0:T(8,128)(2,1)S(1)}, bf16[2048,384]{1,0:T(8,128)(2,1)}, u32[]{:S(2)}) copy-start(bf16[2048,384]{1,0:T(8,128)(2,1)} %param.10) | copy-start | bytes 4718596
  11.9 34.4 %all-to-all-start.1 = ((bf16[8,48,2048]{2,1,0:T(8,128)(2,1)}), bf16[8,48,2048]{2,1,0:T(8,128)(2,1)S(1)}, u32[]{:S(2)}, u32[]{:S(2)}) async-start(bf16[8,48,2048]{2,1,0:T(8,128)(2,1)} %bitcast.27), calls=%async_computation.1 | async-start | bytes 3145728 | tf_op jit(solution)/shard_map/all_to_all | solution.py:464
  20.4 13.7 %collective-permute-start.2 = (bf16[1024,384]{1,0:T(8,128)(2,1)S(1)}, bf16[1024,384]{1,0:T(8,128)(2,1)S(1)}, u32[]{:S(2)}, u32[]{:S(2)}) collective-permute-start(bf16[1024,384]{1,0:T(8,128)(2,1)S(1)} %get-tuple-element.41), channel_id=1, source_target_pairs={{0,8},{8,16},{16,24},{24,32},{32,40},{40,48},{48,56},{56,64},{64,7... | collective-permute-start | bytes 2359304 | tf_op jit(solution)/shard_map/ppermute | solution.py:458
  20.5 13.6 %collective-permute-start.3 = (bf16[1024,384]{1,0:T(8,128)(2,1)S(1)}, bf16[1024,384]{1,0:T(8,128)(2,1)S(1)}, u32[]{:S(2)}, u32[]{:S(2)}) collective-permute-start(bf16[1024,384]{1,0:T(8,128)(2,1)S(1)} %get-tuple-element.40), channel_id=1, source_target_pairs={{8,0},{16,8},{24,16},{32,24},{40,32},{48,40},{56,48},{64,56},{72,6... | collective-permute-start | bytes 2359304 | tf_op jit(solution)/shard_map/ppermute | solution.py:459
  34.1 0.9 copy-start.10
  34.1 1.2 %copy-start.11 = (bf16[1024,384]{1,0:T(8,128)(2,1)}, bf16[1024,384]{1,0:T(8,128)(2,1)S(1)}, u32[]{:S(2)}) copy-start(bf16[1024,384]{1,0:T(8,128)(2,1)S(1)} %collective-permute-done.3) | copy-start | bytes 2359300
  46.2 1.1 %copy-start.6 = (bf16[8,48,2048]{2,1,0:T(8,128)(2,1)}, bf16[8,48,2048]{2,1,0:T(8,128)(2,1)S(1)}, u32[]{:S(2)}) copy-start(bf16[8,48,2048]{2,1,0:T(8,128)(2,1)S(1)} %all-to-all-done.1) | copy-start | bytes 4718596
  47.4 29.2 %all-to-all-start = ((bf16[8,48,2048]{2,1,0:T(8,128)(2,1)}), bf16[8,48,2048]{2,1,0:T(8,128)(2,1)S(1)}, u32[]{:S(2)}, u32[]{:S(2)}) async-start(bf16[8,48,2048]{2,1,0:T(8,128)(2,1)} %bitcast.24), calls=%async_computation | async-start | bytes 3145728 | tf_op jit(solution)/shard_map/all_to_all | solution.py:464
  54.6 22.0 %copy-start.4 = (bf16[384,384]{1,0:T(8,128)(2,1)S(1)}, bf16[384,384]{1,0:T(8,128)(2,1)}, u32[]{:S(2)}) copy-start(bf16[384,384]{1,0:T(8,128)(2,1)} %get-tuple-element.26.back_ref) | copy-start | bytes 884740
  72.6 28.3 %collective-permute-start.4 = (bf16[2,2,4,128,384]{4,3,2,1,0:T(8,128)(2,1)}, bf16[2,2,4,128,384]{4,3,2,1,0:T(8,128)(2,1)S(1)}, u32[]{:S(2)}, u32[]{:S(2)}) collective-permute-start(bf16[2,2,4,128,384]{4,3,2,1,0:T(8,128)(2,1)} %get-tuple-element.35), channel_id=1, source_target_pairs={{0,8},{8,16},{16,24},{24,32},{32,40},{40,48},{48,56},{56,64},{64,7... | collective-permute-start | bytes 4718600 | tf_op jit(solution)/shard_map/ppermute | solution.py:474
  72.7 28.2 %collective-permute-start.5 = (bf16[2,2,4,128,384]{4,3,2,1,0:T(8,128)(2,1)}, bf16[2,2,4,128,384]{4,3,2,1,0:T(8,128)(2,1)}, u32[]{:S(2)}, u32[]{:S(2)}) collective-permute-start(bf16[2,2,4,128,384]{4,3,2,1,0:T(8,128)(2,1)} %get-tuple-element.36), channel_id=1, source_target_pairs={{8,0},{16,8},{24,16},{32,24},{40,32},{48,40},{56,48},{64,56},{72,6... | collective-permute-start | bytes 4718600 | tf_op jit(solution)/shard_map/ppermute | solution.py:475
  76.6 1.4 %copy-start.2 = (bf16[2048,384]{1,0:T(8,128)(2,1)S(1)}, bf16[2048,384]{1,0:T(8,128)(2,1)}, u32[]{:S(2)}) copy-start(bf16[2048,384]{1,0:T(8,128)(2,1)} %param.15) | copy-start | bytes 4718596
  78.0 2.4 %copy-start.9 = (bf16[3,128,128]{2,1,0:T(8,128)(2,1)S(1)}, bf16[3,128,128]{2,1,0:T(8,128)(2,1)}, u32[]{:S(2)}) copy-start(bf16[3,128,128]{2,1,0:T(8,128)(2,1)} %get-tuple-element.39) | copy-start | bytes 294916
  78.0 7.1 %copy-start.3 = (bf16[384,384]{1,0:T(8,128)(2,1)S(1)}, bf16[384,384]{1,0:T(8,128)(2,1)}, u32[]{:S(2)}) copy-start(bf16[384,384]{1,0:T(8,128)(2,1)} %get-tuple-element.23.w_ref) | copy-start | bytes 884740
  80.4 1.4 %collective-permute-start.6 = (bf16[3,128,128]{2,1,0:T(8,128)(2,1)S(1)}, bf16[3,128,128]{2,1,0:T(8,128)(2,1)S(1)}, u32[]{:S(2)}, u32[]{:S(2)}) collective-permute-start(bf16[3,128,128]{2,1,0:T(8,128)(2,1)S(1)} %broadcast_select_fusion), channel_id=1, source_target_pairs={{0,8},{8,0},{16,24},{24,16},{32,40},{40,32},{48,56},{56,48},{64,72... | collective-permute-start | bytes 294920 | tf_op jit(solution)/shard_map/ppermute | solution.py:428
  81.8 17.1 %collective-permute-start.9 = (bf16[3,128,128]{2,1,0:T(8,128)(2,1)S(1)}, bf16[3,128,128]{2,1,0:T(8,128)(2,1)S(1)}, u32[]{:S(2)}, u32[]{:S(2)}) collective-permute-start(bf16[3,128,128]{2,1,0:T(8,128)(2,1)S(1)} %add_convert_fusion.2), channel_id=1, source_target_pairs={{0,48},{8,56},{16,0},{24,8},{32,16},{40,24},{48,32},{56,40},{64,11... | collective-permute-start | bytes 294920 | tf_op jit(solution)/shard_map/ppermute | solution.py:428
  83.6 15.4 %collective-permute-start.8 = (bf16[3,128,128]{2,1,0:T(8,128)(2,1)S(1)}, bf16[3,128,128]{2,1,0:T(8,128)(2,1)S(1)}, u32[]{:S(2)}, u32[]{:S(2)}) collective-permute-start(bf16[3,128,128]{2,1,0:T(8,128)(2,1)S(1)} %add_convert_fusion.2), channel_id=1, source_target_pairs={{0,16},{8,24},{16,32},{24,40},{32,48},{40,56},{48,0},{56,8},{64,80... | collective-permute-start | bytes 294920 | tf_op jit(solution)/shard_map/ppermute | solution.py:428
  83.9 15.0 %collective-permute-start.7 = (bf16[3,128,128]{2,1,0:T(8,128)(2,1)S(1)}, bf16[3,128,128]{2,1,0:T(8,128)(2,1)S(1)}, u32[]{:S(2)}, u32[]{:S(2)}) collective-permute-start(bf16[3,128,128]{2,1,0:T(8,128)(2,1)S(1)} %add_convert_fusion.2), channel_id=1, source_target_pairs={{0,32},{8,40},{16,48},{24,56},{32,0},{40,8},{48,16},{56,24},{64,96... | collective-permute-start | bytes 294920 | tf_op jit(solution)/shard_map/ppermute | solution.py:428
  85.1 15.8 %copy-start.1 = (bf16[4,4,128,384]{3,2,1,0:T(8,128)(2,1)S(1)}, bf16[4,4,128,384]{3,2,1,0:T(8,128)(2,1)}, u32[]{:S(2)}) copy-start(bf16[4,4,128,384]{3,2,1,0:T(8,128)(2,1)} %get-tuple-element.34.dv_ref) | copy-start | bytes 4718596
  88.0 12.9 %copy-start = (bf16[4,4,128,384]{3,2,1,0:T(8,128)(2,1)S(1)}, bf16[4,4,128,384]{3,2,1,0:T(8,128)(2,1)}, u32[]{:S(2)}) copy-start(bf16[4,4,128,384]{3,2,1,0:T(8,128)(2,1)} %get-tuple-element.33.dk_ref) | copy-start | bytes 4718596
  99.6 5.7 %collective-permute-start.10 = (bf16[3,128,128]{2,1,0:T(8,128)(2,1)}, bf16[3,128,128]{2,1,0:T(8,128)(2,1)S(1)}, u32[]{:S(2)}, u32[]{:S(2)}) collective-permute-start(bf16[3,128,128]{2,1,0:T(8,128)(2,1)} %gate.2), channel_id=1, source_target_pairs={{0,64},{8,72},{16,80},{24,88},{32,96},{40,104},{48,112},{56,120},{... | collective-permute-start | bytes 294920 | tf_op jit(solution)/shard_map/ppermute | solution.py:428
  105.3 0.9 copy-start.7
  105.3 0.6 copy-start.8
  107.2 1.4 %collective-permute-start.11 = (bf16[3,128,128]{2,1,0:T(8,128)(2,1)S(1)}, bf16[3,128,128]{2,1,0:T(8,128)(2,1)S(1)}, u32[]{:S(2)}, u32[]{:S(2)}) collective-permute-start(bf16[3,128,128]{2,1,0:T(8,128)(2,1)S(1)} %add_convert_fusion), channel_id=1, source_target_pairs={{0,8},{8,0},{16,24},{24,16},{32,40},{40,32},{48,56},{56,48},{64,72... | collective-permute-start | bytes 294920 | tf_op jit(solution)/shard_map/ppermute | solution.py:428

commit v4 on v3

--- a/solution.py
+++ b/solution.py
@@ -272,16 +272,6 @@
 ):
     lo, hi = (klo, vlo), (khi, vhi)
     t = pl.program_id(0)
-    term = dot(at_ref[...], dm_ref[...], NT)
-
-    @pl.when(t == 0)
-    def _():
-        acc_ref[...] = term
-
-    @pl.when(t > 0)
-    def _():
-        acc_ref[...] += term
-
     dat_all = dot(rb_ref[...], dm_ref[...])
 
     def start(h, pair):
@@ -318,6 +308,16 @@
                 own = low[(e + 2) * TILE : (e + 3) * TILE] + high[e * TILE : (e + 1) * TILE]
                 own_ref[e, 0, :, cols] = own.astype(BF16)
 
+    term = dot(at_ref[...], dm_ref[...], NT)
+
+    @pl.when(t == 0)
+    def _():
+        acc_ref[...] = term
+
+    @pl.when(t > 0)
+    def _():
+        acc_ref[...] += term
+
     @pl.when(t == NTILE - 1)
     def _():
         full = dot(acc_ref[...].astype(BF16), piece_order_t())
@@ -430,15 +430,15 @@
     def along_x(by):
         return lambda i: (i // 8) * 8 + (i % 8 + 2 * by) % 8
 
+    right = gate(right, projected)
     x = jnp.where(first, right, left).astype(F32)
     x = (x + moved(jnp.where(first, left, right), lambda i: i ^ 1).astype(F32)).astype(BF16)
     one, two, three = (moved(x, along_x(by)).astype(F32) for by in (1, 2, 3))
     x = ((x.astype(F32) + two) + (one + three)).astype(BF16)
-    x = gate(x, projected)
-    far = gate(moved(x, lambda i: i ^ 8), dk)
-    x = (x.astype(F32) + far.astype(F32)).astype(BF16)
-    other = moved(x, lambda i: i ^ 1).astype(F32) * norm
-    x = x.astype(F32) * norm
+    near = moved(x, lambda i: i ^ 1).astype(F32)
+    far = gate(moved(x, lambda i: i ^ 8), dk).astype(F32)
+    cross = moved(x, lambda i: i ^ 9).astype(F32)
+    x, other = (x.astype(F32) + far) * norm, (near + cross) * norm
     return jnp.where(first, x, other), jnp.where(first, other, x)
 
 

time: 111 us -> 109 us (0.982)
  waiting for transfers between devices: 20.6 us -> 17 us
  starting transfers between devices: 32 us -> 34.3 us
    ppermute x6 -> x7, waiting for transfers between devices: 13.5 us -> 9.93 us  [moved(): return lax.ppermute(y, 'tm', [(i, to(i)) for i in range(count)])]
    ppermute x6 -> x7, starting transfers between devices: 4.74 us -> 6.96 us  [moved(): return lax.ppermute(y, 'tm', [(i, to(i)) for i in range(count)])]
    unnamed x24 -> x20, local copies, waits for them, and re-layouts: 4.66 us -> 4.38 us
  transfers between devices with their start and end apart: 14 -> 15, of which waited for: 4 -> 3; matrix products, arithmetic and copies ran while one was open for 1% -> 1% of each run, Pallas kernels for 42% -> 42%
where the time goes in v4:
time: 109 us; the launch traced here: 107 us
  Pallas kernels  45.5 us (42%)
  starting transfers between devices  34.3 us (31%)
  waiting for transfers between devices  17 us (16%)
  local copies, waits for them, and re-layouts  7.2 us (7%)
  other arithmetic  2.71 us (2%)
    pallas_call x1, Pallas kernels, backward(): pl.pallas_call(backward_kernel, grid=(NTILE,), in_specs=[tile_spec(FR_DEV...  17.4 us
    all_to_all x2, starting transfers between devices, exchange(): lax.all_to_all(x.reshape(n_head, width // n_head, rows), 'head', split_ax...  15.6 us
    pallas_call x1, Pallas kernels, forward(): pl.pallas_call(forward_kernel, grid=(NTILE,), in_specs=[smem()] + [tile_s...  10.9 us
    ppermute x7, waiting for transfers between devices, moved(): return lax.ppermute(y, 'tm', [(i, to(i)) for i in range(count)])  9.93 us
    ppermute x1, waiting for transfers between devices, on_device(): lax.ppermute(values[rows - cut:], 'tm', up).reshape(half)  7.07 us
    ppermute x7, starting transfers between devices, moved(): return lax.ppermute(y, 'tm', [(i, to(i)) for i in range(count)])  6.96 us
    pallas_call x1, Pallas kernels, prep(): pl.pallas_call(prep_kernel, grid=(NTILE,), in_specs=[smem(), whole((HL, B...  4.7 us
    pallas_call x1, Pallas kernels, add_halos(): pl.pallas_call(add_kernel, grid=(NTILE,), in_specs=[tile_spec(FR_DEV)] *...  4.41 us
  transfers between devices with their start and end apart: 15, of which 3 were waited for; matrix products, arithmetic and copies ran while one was open for 1% of the time, Pallas kernels for 42%

profile of v4, /device:TPU:16, one launch (start us, length us, event | category | flops | bytes accessed | tf_op | source)
XLA Modules:
  0.0 107.4 jit_solution(507080379641039337)
XLA Ops:
  0.6 2.7 %fusion.3 = (bf16[1024,384]{1,0:T(8,128)(2,1)}, bf16[1024,384]{1,0:T(8,128)(2,1)}) fusion(bf16[2048,384]{1,0:T(8,128)(2,1)} %param.9), kind=kLoop, calls=%fused_computation.8 | loop fusion | bytes 3145728 | tf_op jit(solution)/shard_map/slice | solution.py:457
  3.3 0.0 collective-permute-start
  3.3 3.9 %collective-permute-start.1 = (bf16[1024,384]{1,0:T(8,128)(2,1)}, bf16[1024,384]{1,0:T(8,128)(2,1)}, u32[]{:S(2)}, u32[]{:S(2)}) collective-permute-start(bf16[1024,384]{1,0:T(8,128)(2,1)} %get-tuple-element.42), channel_id=1, source_target_pairs={{8,0},{16,8},{24,16},{32,24},{40,32},{48,40},{56,48},{64,56},{72,6... | collective-permute-start | bytes 2359304 | tf_op jit(solution)/shard_map/ppermute | solution.py:457
  7.2 4.7 %prep.1 = (bf16[384,384]{1,0:T(8,128)(2,1)}, bf16[384,2048]{1,0:T(8,128)(2,1)}) custom-call(s32[24]{0:T(128)} %perm_ref.3, bf16[3,128,128]{2,1,0:T(8,128)(2,1)} %left_ref.1, bf16[4,4,128,384]{3,2,1,0:T(8,128)(2,1)} %bitcast.18), custom_call_target="tpu_custom_call" | custom-call | flops 1000000000 | bytes 4000000 | tf_op jit(solution)/shard_map/prep/pallas_call | solution.py:139
  11.9 0.0 copy-start.5
  11.9 8.4 %all-to-all-start.1 = ((bf16[8,48,2048]{2,1,0:T(8,128)(2,1)}), bf16[8,48,2048]{2,1,0:T(8,128)(2,1)S(1)}, u32[]{:S(2)}, u32[]{:S(2)}) async-start(bf16[8,48,2048]{2,1,0:T(8,128)(2,1)} %bitcast.27), calls=%async_computation.1 | async-start | bytes 3145728 | tf_op jit(solution)/shard_map/all_to_all | solution.py:464
  20.3 0.0 copy-done.5
  20.3 0.2 fusion.2
  20.4 0.1 collective-permute-start.2
  20.5 3.8 %collective-permute-start.3 = (bf16[1024,384]{1,0:T(8,128)(2,1)S(1)}, bf16[1024,384]{1,0:T(8,128)(2,1)S(1)}, u32[]{:S(2)}, u32[]{:S(2)}) collective-permute-start(bf16[1024,384]{1,0:T(8,128)(2,1)S(1)} %get-tuple-element.40), channel_id=1, source_target_pairs={{8,0},{16,8},{24,16},{32,24},{40,32},{48,40},{56,48},{64,56},{72,6... | collective-permute-start | bytes 2359304 | tf_op jit(solution)/shard_map/ppermute | solution.py:459
  24.4 2.7 %orders.1 = (bf16[384,384]{1,0:T(8,128)(2,1)}, bf16[384,384]{1,0:T(8,128)(2,1)}, bf16[384,384]{1,0:T(8,128)(2,1)}) custom-call(s32[24]{0:T(128)} %perm_ref.3, bf16[3,128,128]{2,1,0:T(8,128)(2,1)} %right_ref.1), custom_call_target="tpu_custom_call" | custom-call | flops 300000000 | bytes 1000000 | tf_op jit(solution)/shard_map/orders/pallas_call | solution.py:163
  27.1 0.0 collective-permute-done
  27.1 0.0 collective-permute-done.1
  27.1 7.1 %collective-permute-done.2 = bf16[1024,384]{1,0:T(8,128)(2,1)S(1)} collective-permute-done((bf16[1024,384]{1,0:T(8,128)(2,1)S(1)}, bf16[1024,384]{1,0:T(8,128)(2,1)S(1)}, u32[]{:S(2)}, u32[]{:S(2)}) %collective-permute-start.2) | collective-permute-done | bytes 786464 | tf_op jit(solution)/shard_map/ppermute | solution.py:458
  34.1 0.0 copy-start.8
  34.1 0.0 collective-permute-done.3
  34.1 0.0 copy-start.9
  34.1 0.9 copy-done.8
  35.0 0.3 copy-done.9
  35.3 10.9 %forward.1 = (bf16[384,2048]{1,0:T(8,128)(2,1)}, bf16[4,3,2,768,256]{4,3,2,1,0:T(8,128)(2,1)}, f32[4,8,512]{2,1,0:T(8,128)}, bf16[384,2048]{1,0:T(8,128)(2,1)}) custom-call(s32[24]{0:T(128)} %reach_ref.1, bf16[4,4,128,384]{3,2,1,0:T(8,128)(2,1)} %bitcast.29, bf16[4,4,128,384]{3,2,1,0:T(8,128)(2,1)} %bitcast.20, bf16[4,4,128,384]{3,2,1,0:T(8,128)(2,1)} %bitcast.22, ...), custom_call_target="tpu_custom_call" | custom-call | flops 6000000000 | bytes 20000000 | tf_op jit(solution)/shard_map/forward/pallas_call | solution.py:247
  46.2 0.0 all-to-all-done.1
  46.2 0.0 copy-start.6
  46.2 1.1 %copy-done.6 = bf16[8,48,2048]{2,1,0:T(8,128)(2,1)} copy-done((bf16[8,48,2048]{2,1,0:T(8,128)(2,1)}, bf16[8,48,2048]{2,1,0:T(8,128)(2,1)S(1)}, u32[]{:S(2)}) %copy-start.6) | copy-done | bytes 1572888
  47.4 7.2 %all-to-all-start = ((bf16[8,48,2048]{2,1,0:T(8,128)(2,1)}), bf16[8,48,2048]{2,1,0:T(8,128)(2,1)S(1)}, u32[]{:S(2)}, u32[]{:S(2)}) async-start(bf16[8,48,2048]{2,1,0:T(8,128)(2,1)} %bitcast.25), calls=%async_computation | async-start | bytes 3145728 | tf_op jit(solution)/shard_map/all_to_all | solution.py:464
  54.6 0.0 copy-start.4
  54.6 17.4 %backward.1 = (bf16[4,4,128,384]{3,2,1,0:T(8,128)(2,1)}, bf16[4,4,128,384]{3,2,1,0:T(8,128)(2,1)}, bf16[4,4,128,384]{3,2,1,0:T(8,128)(2,1)}, bf16[2,2,4,128,384]...) custom-call(bf16[4,4,128,384]{3,2,1,0:T(8,128)(2,1)} %bitcast.30, ...), custom_call_target="tpu_custom_call" | custom-call | flops 12000000000 | bytes 30000000 | tf_op jit(solution)/shard_map/backward/pallas_call | solution.py:332
  72.0 0.1 collective-permute-start.4
  72.1 3.8 %collective-permute-start.5 = (bf16[2,2,4,128,384]{4,3,2,1,0:T(8,128)(2,1)}, bf16[2,2,4,128,384]{4,3,2,1,0:T(8,128)(2,1)}, u32[]{:S(2)}, u32[]{:S(2)}) collective-permute-start(bf16[2,2,4,128,384]{4,3,2,1,0:T(8,128)(2,1)} %get-tuple-element.36), channel_id=1, source_target_pairs={{8,0},{16,8},{24,16},{32,24},{40,32},{48,40},{56,48},{64,56},{72,6... | collective-permute-start | bytes 4718600 | tf_op jit(solution)/shard_map/ppermute | solution.py:475
  76.0 0.0 all-to-all-done
  76.0 0.0 copy-done.4
  76.0 0.0 copy-start.2
  76.0 1.4 %copy-done.2 = bf16[2048,384]{1,0:T(8,128)(2,1)S(1)} copy-done((bf16[2048,384]{1,0:T(8,128)(2,1)S(1)}, bf16[2048,384]{1,0:T(8,128)(2,1)}, u32[]{:S(2)}) %copy-start.2) | copy-done | bytes 1572888
  77.4 0.0 copy-start.3
  77.4 2.4 %left_sum.1._ = bf16[3,128,128]{2,1,0:T(8,128)(2,1)S(1)} custom-call(bf16[384,384]{1,0:T(8,128)(2,1)S(1)} %copy-done.4, bf16[384,2048]{1,0:T(8,128)(2,1)S(1)} %bitcast.16, bf16[4,4,128,384]{3,2,1,0:T(8,128)(2,1)S(1)} %bitcast.19), custom_call_target="tpu_custom_call" | custom-call | flops 1000000000 | bytes 4000000 | tf_op jit(solution)/shard_map/left_sum/pallas_call | solution.py:390
  79.7 0.0 copy-done.3
  79.8 0.0 copy-start.1
  79.8 2.9 %project.1.refs_1_ = bf16[4,4,128,384]{3,2,1,0:T(8,128)(2,1)} custom-call(bf16[384,384]{1,0:T(8,128)(2,1)S(1)} %copy-done.3, bf16[384,2048]{1,0:T(8,128)(2,1)S(1)} %bitcast.17, bf16[3,128,128]{2,1,0:T(8,128)(2,1)S(1)} %left_sum.1._), custom_call_target="tpu_custom_call" | custom-call | flops 1000000000 | bytes 4000000 | tf_op jit(solution)/shard_map/project/pallas_call | solution.py:411
  82.7 0.0 copy-start
  82.7 0.1 collective-permute-start.6
  82.8 1.3 %collective-permute-done.6 = bf16[3,128,128]{2,1,0:T(8,128)(2,1)S(1)} collective-permute-done((bf16[3,128,128]{2,1,0:T(8,128)(2,1)S(1)}, bf16[3,128,128]{2,1,0:T(8,128)(2,1)S(1)}, u32[]{:S(2)}, u32[]{:S(2)}) %collective-permute-start.6) | collective-permute-done | bytes 98336 | tf_op jit(solution)/shard_map/ppermute | solution.py:428
  84.1 0.9 add_convert_fusion.1
  85.0 3.1 %collective-permute-start.9 = (bf16[3,128,128]{2,1,0:T(8,128)(2,1)S(1)}, bf16[3,128,128]{2,1,0:T(8,128)(2,1)S(1)}, u32[]{:S(2)}, u32[]{:S(2)}) collective-permute-start(bf16[3,128,128]{2,1,0:T(8,128)(2,1)S(1)} %add_convert_fusion.1), channel_id=1, source_target_pairs={{0,48},{8,56},{16,0},{24,8},{32,16},{40,24},{48,32},{56,40},{64,11... | collective-permute-start | bytes 294920 | tf_op jit(solution)/shard_map/ppermute | solution.py:428
  88.2 0.0 collective-permute-start.8
  88.2 1.5 %collective-permute-start.7 = (bf16[3,128,128]{2,1,0:T(8,128)(2,1)S(1)}, bf16[3,128,128]{2,1,0:T(8,128)(2,1)S(1)}, u32[]{:S(2)}, u32[]{:S(2)}) collective-permute-start(bf16[3,128,128]{2,1,0:T(8,128)(2,1)S(1)} %add_convert_fusion.1), channel_id=1, source_target_pairs={{0,32},{8,40},{16,48},{24,56},{32,0},{40,8},{48,16},{56,24},{64,96... | collective-permute-start | bytes 294920 | tf_op jit(solution)/shard_map/ppermute | solution.py:428
  89.7 8.6 %collective-permute-done.9 = bf16[3,128,128]{2,1,0:T(8,128)(2,1)S(1)} collective-permute-done((bf16[3,128,128]{2,1,0:T(8,128)(2,1)S(1)}, bf16[3,128,128]{2,1,0:T(8,128)(2,1)S(1)}, u32[]{:S(2)}, u32[]{:S(2)}) %collective-permute-start.9) | collective-permute-done | bytes 98336 | tf_op jit(solution)/shard_map/ppermute | solution.py:428
  98.3 0.0 collective-permute-done.8
  98.3 0.0 collective-permute-done.7
  98.3 0.1 add_convert_fusion
  98.4 1.4 %collective-permute-start.10 = (bf16[3,128,128]{2,1,0:T(8,128)(2,1)S(1)}, bf16[3,128,128]{2,1,0:T(8,128)(2,1)S(1)}, u32[]{:S(2)}, u32[]{:S(2)}) collective-permute-start(bf16[3,128,128]{2,1,0:T(8,128)(2,1)S(1)} %add_convert_fusion), channel_id=1, source_target_pairs={{0,64},{8,72},{16,80},{24,88},{32,96},{40,104},{48,112},{56,120},{... | collective-permute-start | bytes 294920 | tf_op jit(solution)/shard_map/ppermute | solution.py:428
  99.8 0.0 collective-permute-start.12
  99.8 0.9 collective-permute-start.11
  100.6 0.0 collective-permute-done.4.below_ref
  100.6 0.0 collective-permute-done.5.above_ref
  100.6 0.0 copy-done.1
  100.6 0.0 copy-done
  100.6 4.4 %add_halos.1 = (bf16[4,4,128,384]{3,2,1,0:T(8,128)(2,1)}, bf16[4,4,128,384]{3,2,1,0:T(8,128)(2,1)}) custom-call(bf16[4,4,128,384]{3,2,1,0:T(8,128)(2,1)S(1)} %copy-done, bf16[4,4,128,384]{3,2,1,0:T(8,128)(2,1)S(1)} %copy-done.1, bf16[2,2,4,128,384]{4,3,2,1,0:T(8,128)(2,1)S(1)} %collective-permute-done.4.below_ref, ...), custom_call_target="tpu_custom_call" | custom-call | flops 1000000 | bytes 10000000 | tf_op jit(solution)/shard_map/add_halos/pallas_call | solution.py:358
  105.1 0.0 collective-permute-done.10.refs_0_
  105.1 0.0 copy-start.7
  105.1 0.6 copy-done.7
  105.7 0.0 collective-permute-done.12
  105.7 0.0 collective-permute-done.11
  105.7 1.7 %fusion = (f32[3,128,128]{2,1,0:T(8,128)}, f32[3,128,128]{2,1,0:T(8,128)}) fusion(bf16[3,128,128]{2,1,0:T(8,128)(2,1)} %gate.3, bf16[3,128,128]{2,1,0:T(8,128)(2,1)S(1)} %add_convert_fusion, bf16[3,128,128]{2,1,0:T(8,128)(2,1)S(1)} %collective-permute-done.12, bf16[3,128,128]{2,1,0:T(8,128)(2,1)S(1)} %collective-permute-done.11, pred[]{:T(512)S(6)} %eq.5), kind=kLoop, calls=%fused_computation.4 | loop fusion | flops 491520 | bytes 786433 | tf_op jit(solution)/shard_map/jit(_where)/select_n | solution.py:442
  (3 shorter events, 0.0 us)
Async XLA Ops:
  3.3 23.8 %collective-permute-start = (bf16[1024,384]{1,0:T(8,128)(2,1)}, bf16[1024,384]{1,0:T(8,128)(2,1)}, u32[]{:S(2)}, u32[]{:S(2)}) collective-permute-start(bf16[1024,384]{1,0:T(8,128)(2,1)} %get-tuple-element.43), channel_id=1, source_target_pairs={{0,8},{8,16},{16,24},{24,32},{32,40},{40,48},{48,56},{56,64},{64,7... | collective-permute-start | bytes 2359304 | tf_op jit(solution)/shard_map/ppermute | solution.py:456
  3.3 23.8 %collective-permute-start.1 = (bf16[1024,384]{1,0:T(8,128)(2,1)}, bf16[1024,384]{1,0:T(8,128)(2,1)}, u32[]{:S(2)}, u32[]{:S(2)}) collective-permute-start(bf16[1024,384]{1,0:T(8,128)(2,1)} %get-tuple-element.42), channel_id=1, source_target_pairs={{8,0},{16,8},{24,16},{32,24},{40,32},{48,40},{56,48},{64,56},{72,6... | collective-permute-start | bytes 2359304 | tf_op jit(solution)/shard_map/ppermute | solution.py:457
  11.9 8.4 %copy-start.5 = (bf16[2048,384]{1,0:T(8,128)(2,1)S(1)}, bf16[2048,384]{1,0:T(8,128)(2,1)}, u32[]{:S(2)}) copy-start(bf16[2048,384]{1,0:T(8,128)(2,1)} %param.10) | copy-start | bytes 4718596
  11.9 34.4 %all-to-all-start.1 = ((bf16[8,48,2048]{2,1,0:T(8,128)(2,1)}), bf16[8,48,2048]{2,1,0:T(8,128)(2,1)S(1)}, u32[]{:S(2)}, u32[]{:S(2)}) async-start(bf16[8,48,2048]{2,1,0:T(8,128)(2,1)} %bitcast.27), calls=%async_computation.1 | async-start | bytes 3145728 | tf_op jit(solution)/shard_map/all_to_all | solution.py:464
  20.4 13.7 %collective-permute-start.2 = (bf16[1024,384]{1,0:T(8,128)(2,1)S(1)}, bf16[1024,384]{1,0:T(8,128)(2,1)S(1)}, u32[]{:S(2)}, u32[]{:S(2)}) collective-permute-start(bf16[1024,384]{1,0:T(8,128)(2,1)S(1)} %get-tuple-element.41), channel_id=1, source_target_pairs={{0,8},{8,16},{16,24},{24,32},{32,40},{40,48},{48,56},{56,64},{64,7... | collective-permute-start | bytes 2359304 | tf_op jit(solution)/shard_map/ppermute | solution.py:458
  20.5 13.6 %collective-permute-start.3 = (bf16[1024,384]{1,0:T(8,128)(2,1)S(1)}, bf16[1024,384]{1,0:T(8,128)(2,1)S(1)}, u32[]{:S(2)}, u32[]{:S(2)}) collective-permute-start(bf16[1024,384]{1,0:T(8,128)(2,1)S(1)} %get-tuple-element.40), channel_id=1, source_target_pairs={{8,0},{16,8},{24,16},{32,24},{40,32},{48,40},{56,48},{64,56},{72,6... | collective-permute-start | bytes 2359304 | tf_op jit(solution)/shard_map/ppermute | solution.py:459
  34.1 0.9 copy-start.8
  34.1 1.2 %copy-start.9 = (bf16[1024,384]{1,0:T(8,128)(2,1)}, bf16[1024,384]{1,0:T(8,128)(2,1)S(1)}, u32[]{:S(2)}) copy-start(bf16[1024,384]{1,0:T(8,128)(2,1)S(1)} %collective-permute-done.3) | copy-start | bytes 2359300
  46.2 1.1 %copy-start.6 = (bf16[8,48,2048]{2,1,0:T(8,128)(2,1)}, bf16[8,48,2048]{2,1,0:T(8,128)(2,1)S(1)}, u32[]{:S(2)}) copy-start(bf16[8,48,2048]{2,1,0:T(8,128)(2,1)S(1)} %all-to-all-done.1) | copy-start | bytes 4718596
  47.4 28.6 %all-to-all-start = ((bf16[8,48,2048]{2,1,0:T(8,128)(2,1)}), bf16[8,48,2048]{2,1,0:T(8,128)(2,1)S(1)}, u32[]{:S(2)}, u32[]{:S(2)}) async-start(bf16[8,48,2048]{2,1,0:T(8,128)(2,1)} %bitcast.25), calls=%async_computation | async-start | bytes 3145728 | tf_op jit(solution)/shard_map/all_to_all | solution.py:464
  54.6 21.4 %copy-start.4 = (bf16[384,384]{1,0:T(8,128)(2,1)S(1)}, bf16[384,384]{1,0:T(8,128)(2,1)}, u32[]{:S(2)}) copy-start(bf16[384,384]{1,0:T(8,128)(2,1)} %get-tuple-element.26.back_ref) | copy-start | bytes 884740
  72.0 28.6 %collective-permute-start.4 = (bf16[2,2,4,128,384]{4,3,2,1,0:T(8,128)(2,1)}, bf16[2,2,4,128,384]{4,3,2,1,0:T(8,128)(2,1)S(1)}, u32[]{:S(2)}, u32[]{:S(2)}) collective-permute-start(bf16[2,2,4,128,384]{4,3,2,1,0:T(8,128)(2,1)} %get-tuple-element.35), channel_id=1, source_target_pairs={{0,8},{8,16},{16,24},{24,32},{32,40},{40,48},{48,56},{56,64},{64,7... | collective-permute-start | bytes 4718600 | tf_op jit(solution)/shard_map/ppermute | solution.py:474
  72.1 28.5 %collective-permute-start.5 = (bf16[2,2,4,128,384]{4,3,2,1,0:T(8,128)(2,1)}, bf16[2,2,4,128,384]{4,3,2,1,0:T(8,128)(2,1)}, u32[]{:S(2)}, u32[]{:S(2)}) collective-permute-start(bf16[2,2,4,128,384]{4,3,2,1,0:T(8,128)(2,1)} %get-tuple-element.36), channel_id=1, source_target_pairs={{8,0},{16,8},{24,16},{32,24},{40,32},{48,40},{56,48},{64,56},{72,6... | collective-permute-start | bytes 4718600 | tf_op jit(solution)/shard_map/ppermute | solution.py:475
  76.0 1.4 %copy-start.2 = (bf16[2048,384]{1,0:T(8,128)(2,1)S(1)}, bf16[2048,384]{1,0:T(8,128)(2,1)}, u32[]{:S(2)}) copy-start(bf16[2048,384]{1,0:T(8,128)(2,1)} %param.15) | copy-start | bytes 4718596
  77.4 2.4 %copy-start.3 = (bf16[384,384]{1,0:T(8,128)(2,1)S(1)}, bf16[384,384]{1,0:T(8,128)(2,1)}, u32[]{:S(2)}) copy-start(bf16[384,384]{1,0:T(8,128)(2,1)} %get-tuple-element.23.w_ref) | copy-start | bytes 884740
  79.8 20.9 %copy-start.1 = (bf16[4,4,128,384]{3,2,1,0:T(8,128)(2,1)S(1)}, bf16[4,4,128,384]{3,2,1,0:T(8,128)(2,1)}, u32[]{:S(2)}) copy-start(bf16[4,4,128,384]{3,2,1,0:T(8,128)(2,1)} %get-tuple-element.34.dv_ref) | copy-start | bytes 4718596
  82.7 17.9 %copy-start = (bf16[4,4,128,384]{3,2,1,0:T(8,128)(2,1)S(1)}, bf16[4,4,128,384]{3,2,1,0:T(8,128)(2,1)}, u32[]{:S(2)}) copy-start(bf16[4,4,128,384]{3,2,1,0:T(8,128)(2,1)} %get-tuple-element.33.dk_ref) | copy-start | bytes 4718596
  82.7 1.4 %collective-permute-start.6 = (bf16[3,128,128]{2,1,0:T(8,128)(2,1)S(1)}, bf16[3,128,128]{2,1,0:T(8,128)(2,1)S(1)}, u32[]{:S(2)}, u32[]{:S(2)}) collective-permute-start(bf16[3,128,128]{2,1,0:T(8,128)(2,1)S(1)} %broadcast_select_fusion), channel_id=1, source_target_pairs={{0,8},{8,0},{16,24},{24,16},{32,40},{40,32},{48,56},{56,48},{64,72... | collective-permute-start | bytes 294920 | tf_op jit(solution)/shard_map/ppermute | solution.py:428
  85.0 13.3 %collective-permute-start.9 = (bf16[3,128,128]{2,1,0:T(8,128)(2,1)S(1)}, bf16[3,128,128]{2,1,0:T(8,128)(2,1)S(1)}, u32[]{:S(2)}, u32[]{:S(2)}) collective-permute-start(bf16[3,128,128]{2,1,0:T(8,128)(2,1)S(1)} %add_convert_fusion.1), channel_id=1, source_target_pairs={{0,48},{8,56},{16,0},{24,8},{32,16},{40,24},{48,32},{56,40},{64,11... | collective-permute-start | bytes 294920 | tf_op jit(solution)/shard_map/ppermute | solution.py:428
  88.2 10.2 %collective-permute-start.8 = (bf16[3,128,128]{2,1,0:T(8,128)(2,1)S(1)}, bf16[3,128,128]{2,1,0:T(8,128)(2,1)S(1)}, u32[]{:S(2)}, u32[]{:S(2)}) collective-permute-start(bf16[3,128,128]{2,1,0:T(8,128)(2,1)S(1)} %add_convert_fusion.1), channel_id=1, source_target_pairs={{0,16},{8,24},{16,32},{24,40},{32,48},{40,56},{48,0},{56,8},{64,80... | collective-permute-start | bytes 294920 | tf_op jit(solution)/shard_map/ppermute | solution.py:428
  88.2 10.2 %collective-permute-start.7 = (bf16[3,128,128]{2,1,0:T(8,128)(2,1)S(1)}, bf16[3,128,128]{2,1,0:T(8,128)(2,1)S(1)}, u32[]{:S(2)}, u32[]{:S(2)}) collective-permute-start(bf16[3,128,128]{2,1,0:T(8,128)(2,1)S(1)} %add_convert_fusion.1), channel_id=1, source_target_pairs={{0,32},{8,40},{16,48},{24,56},{32,0},{40,8},{48,16},{56,24},{64,96... | collective-permute-start | bytes 294920 | tf_op jit(solution)/shard_map/ppermute | solution.py:428
  98.4 6.7 %collective-permute-start.10 = (bf16[3,128,128]{2,1,0:T(8,128)(2,1)S(1)}, bf16[3,128,128]{2,1,0:T(8,128)(2,1)S(1)}, u32[]{:S(2)}, u32[]{:S(2)}) collective-permute-start(bf16[3,128,128]{2,1,0:T(8,128)(2,1)S(1)} %add_convert_fusion), channel_id=1, source_target_pairs={{0,64},{8,72},{16,80},{24,88},{32,96},{40,104},{48,112},{56,120},{... | collective-permute-start | bytes 294920 | tf_op jit(solution)/shard_map/ppermute | solution.py:428
  99.8 5.9 %collective-permute-start.12 = (bf16[3,128,128]{2,1,0:T(8,128)(2,1)S(1)}, bf16[3,128,128]{2,1,0:T(8,128)(2,1)S(1)}, u32[]{:S(2)}, u32[]{:S(2)}) collective-permute-start(bf16[3,128,128]{2,1,0:T(8,128)(2,1)S(1)} %add_convert_fusion), channel_id=1, source_target_pairs={{0,72},{8,64},{16,88},{24,80},{32,104},{40,96},{48,120},{56,112},{... | collective-permute-start | bytes 294920 | tf_op jit(solution)/shard_map/ppermute | solution.py:428
  99.8 5.9 %collective-permute-start.11 = (bf16[3,128,128]{2,1,0:T(8,128)(2,1)S(1)}, bf16[3,128,128]{2,1,0:T(8,128)(2,1)S(1)}, u32[]{:S(2)}, u32[]{:S(2)}) collective-permute-start(bf16[3,128,128]{2,1,0:T(8,128)(2,1)S(1)} %add_convert_fusion), channel_id=1, source_target_pairs={{0,8},{8,0},{16,24},{24,16},{32,40},{40,32},{48,56},{56,48},{64,72... | collective-permute-start | bytes 294920 | tf_op jit(solution)/shard_map/ppermute | solution.py:428
  105.1 0.6 copy-start.7
